TPU v7x, 128 devices: a whole 4x4x4 slice. The times are simulated.
128 devices in a mesh: dp: 4 (over y), ctx: 32 (over z, x, core).
Axes of the slice: x: 4, y: 4, z: 4, core: 2. Of those that a mesh axis runs over, the one named last changes fastest.
Arguments:
- queries: bfloat16 [4, 8192, 1024], P('dp', 'ctx'), may hold values from -36 to 36
- key_rows: bfloat16 [4, 8192, 128], P('dp', 'ctx'), may hold values from -12 to 12
- value_rows: bfloat16 [4, 8192, 128], P('dp', 'ctx'), may hold values from -6 to 6
- forward_out: bfloat16 [4, 8192, 1024], P('dp', 'ctx'), may hold values from -6 to 6
- out_grad: bfloat16 [4, 8192, 1024], P('dp', 'ctx'), may hold values from -6 to 6
- layer_input: bfloat16 [4, 8192, 4096], P('dp', 'ctx'), may hold values from -0.21875 to 0.21875
- doc_lengths: int32 [4, 4], P('dp'), may hold values from 1 to 4096, 8192 in all within a row
- held_span: int32 [4, 32], P('dp'), may hold values from 0 to 31, each once within a row
Outputs:
- query_grad: bfloat16 [4, 8192, 1024], P('dp', 'ctx')
- key_grad: bfloat16 [4, 8192, 128], P('dp', 'ctx')
- value_grad: bfloat16 [4, 8192, 128], P('dp', 'ctx')
- weight_grad: float32 [4096, 1280], P(('dp', 'ctx'))
Inputs may be any that keep to these rules, and one draw needn't show every extreme that they name: `doc_lengths`: each row sums to 8192. `held_span`: each row holds every number of 0 to 31 once.
All inputs are finite; a program needn't handle non-finite values.
Results may differ from a plain program's by a relative error of at most 0.011.
Values may be sent and summed in bfloat16 or wider, within the bound.
A program may use at most 128 MiB of HBM per device.

v0:
```python
import math

import jax
import jax.numpy as jnp
from jax import lax
from jax.sharding import PartitionSpec as P

MASK_FILL = -1e30


def document_of(positions, doc_ends):
    return jnp.sum((positions[:, None] >= doc_ends[None, :]).astype(jnp.int32), axis=1)


def row_products(grad_rows, out_rows, head_count, head_dim):
    products = grad_rows.astype(jnp.float32) * out_rows.astype(jnp.float32)
    return jnp.sum(products.reshape(-1, head_count, head_dim), axis=2)


def attend(query_rows, grad_rows, row_delta, positions, keys_seq, doc_ends, head_count, head_dim):
    row_count = query_rows.shape[0]
    seq_tokens = keys_seq.shape[0]
    tile_rows = min(64, row_count)
    key_block = min(512, seq_tokens)
    tile_count = row_count // tile_rows
    block_count = seq_tokens // key_block
    row_width = head_count * head_dim
    logit_scale = 1.0 / math.sqrt(head_dim)
    key_docs = document_of(jnp.arange(seq_tokens, dtype=jnp.int32), doc_ends)

    def block_visible(block_index, tile_pos, tile_doc):
        key_pos = block_index * key_block + jnp.arange(key_block, dtype=jnp.int32)
        block_doc = lax.dynamic_slice_in_dim(key_docs, block_index * key_block, key_block, 0)
        return (block_doc[None, :] == tile_doc[:, None]) & (key_pos[None, :] <= tile_pos[:, None])

    def per_tile(kv_grads, pieces):
        tile_query, tile_grad, tile_delta, tile_pos = pieces
        tile_doc = document_of(tile_pos, doc_ends)
        query_flat = tile_query.reshape(tile_rows * head_count, head_dim)
        grad_flat = tile_grad.reshape(tile_rows * head_count, head_dim)

        def block_logits(block_index):
            kv_block = lax.dynamic_slice_in_dim(keys_seq, block_index * key_block, key_block, 0)
            logits = jnp.einsum(
                "qd,kd->qk", query_flat, kv_block[:, :head_dim], preferred_element_type=jnp.float32
            )
            return ((logits * logit_scale).reshape(tile_rows, head_count, key_block), kv_block)

        def stat_step(block_index, carried):
            visible = block_visible(block_index, tile_pos, tile_doc)

            def stat_update(carried):
                running_max, summed = carried
                logits, kv_block = block_logits(block_index)
                masked = jnp.where(visible[:, None, :], logits, MASK_FILL)
                new_max = jnp.maximum(running_max, jnp.max(masked, axis=2))
                terms = jnp.where(visible[:, None, :], jnp.exp(masked - new_max[:, :, None]), 0.0)
                return (new_max, summed * jnp.exp(running_max - new_max) + jnp.sum(terms, axis=2))

            return lax.cond(jnp.any(visible), stat_update, lambda kept: kept, carried)

        start_state = (
            jnp.full((tile_rows, head_count), MASK_FILL, jnp.float32),
            jnp.zeros((tile_rows, head_count), jnp.float32),
        )
        running_max, summed = lax.fori_loop(0, block_count, stat_step, start_state)
        log_norm = running_max + jnp.log(summed)

        def grad_step(block_index, carried):
            visible = block_visible(block_index, tile_pos, tile_doc)

            def grad_update(carried):
                query_acc, kv_acc = carried
                logits, kv_block = block_logits(block_index)
                probs = jnp.where(visible[:, None, :], jnp.exp(logits - log_norm[:, :, None]), 0.0)
                probs_low = probs.reshape(tile_rows * head_count, key_block).astype(jnp.bfloat16)
                prob_grad = jnp.einsum(
                    "qd,kd->qk",
                    grad_flat,
                    kv_block[:, head_dim:],
                    preferred_element_type=jnp.float32,
                )
                prob_grad = prob_grad.reshape(tile_rows, head_count, key_block)
                logit_grad = probs * (prob_grad - tile_delta[:, :, None])
                logit_grad = logit_grad.reshape(tile_rows * head_count, key_block).astype(
                    jnp.bfloat16
                )
                query_acc = query_acc + jnp.dot(
                    logit_grad, kv_block[:, :head_dim], preferred_element_type=jnp.float32
                )
                key_term = jnp.einsum(
                    "qk,qd->kd", logit_grad, query_flat, preferred_element_type=jnp.float32
                )
                value_term = jnp.einsum(
                    "qk,qd->kd", probs_low, grad_flat, preferred_element_type=jnp.float32
                )
                previous = lax.dynamic_slice_in_dim(kv_acc, block_index * key_block, key_block, 0)
                kv_acc = lax.dynamic_update_slice_in_dim(
                    kv_acc,
                    previous + jnp.concatenate([key_term, value_term], axis=1),
                    block_index * key_block,
                    0,
                )
                return (query_acc, kv_acc)

            return lax.cond(jnp.any(visible), grad_update, lambda kept: kept, carried)

        start_query = jnp.zeros((tile_rows * head_count, head_dim), jnp.float32)
        query_acc, kv_grads = lax.fori_loop(0, block_count, grad_step, (start_query, kv_grads))
        tile_result = (logit_scale * query_acc).reshape(tile_rows, row_width).astype(jnp.bfloat16)
        return (kv_grads, tile_result)

    pieces = (
        query_rows.reshape(tile_count, tile_rows, row_width),
        grad_rows.reshape(tile_count, tile_rows, row_width),
        row_delta.reshape(tile_count, tile_rows, head_count),
        positions.reshape(tile_count, tile_rows),
    )
    start_grads = jnp.zeros((seq_tokens, 2 * head_dim), jnp.float32)
    kv_grads, query_grads = lax.scan(per_tile, start_grads, pieces)
    return (query_grads.reshape(row_count, row_width), kv_grads)


def local(
    queries, key_rows, value_rows, forward_out, out_grad, layer_input, doc_lengths, held_span
):
    tokens_here = queries.shape[1]
    row_width = queries.shape[2]
    head_dim = key_rows.shape[2]
    head_count = row_width // head_dim
    logit_scale = 1.0 / math.sqrt(head_dim)
    ctx_count = lax.axis_size("ctx")
    my_index = lax.axis_index("ctx")
    doc_ends = jnp.cumsum(doc_lengths[0])
    holding = held_span[0]
    device_ids = jnp.arange(ctx_count, dtype=jnp.int32)
    inverse = jnp.sum(
        jnp.where(holding[None, :] == device_ids[:, None], device_ids[None, :], 0), axis=1
    )
    stacked = jnp.concatenate([key_rows[0], value_rows[0]], axis=1)
    gathered = lax.all_gather(stacked, "ctx", axis=0, tiled=True)
    keys_seq = jnp.take(gathered.reshape(ctx_count, tokens_here, 2 * head_dim), inverse, axis=0)
    keys_seq = keys_seq.reshape(ctx_count * tokens_here, 2 * head_dim)
    own_pos = holding[my_index] * tokens_here + jnp.arange(tokens_here, dtype=jnp.int32)
    own_delta = row_products(out_grad[0], forward_out[0], head_count, head_dim)
    query_local, kv_grads = attend(
        queries[0], out_grad[0], own_delta, own_pos, keys_seq, doc_ends, head_count, head_dim
    )
    device_grads = jnp.take(kv_grads.reshape(ctx_count, tokens_here, 2 * head_dim), holding, axis=0)
    device_grads = device_grads.reshape(ctx_count * tokens_here, 2 * head_dim)
    own_sums = lax.psum_scatter(device_grads, "ctx", scatter_dimension=0, tiled=True)
    key_local = (logit_scale * own_sums[:, :head_dim]).astype(jnp.bfloat16)
    value_local = own_sums[:, head_dim:].astype(jnp.bfloat16)
    joined = jnp.concatenate([query_local, key_local, value_local], axis=1)
    input_rows = layer_input[0]
    weight_grad = lax.psum_scatter(
        lax.dot_general(
            input_rows, joined, (((0,), (0,)), ((), ())), preferred_element_type=jnp.float32
        ),
        ("dp", "ctx"),
        scatter_dimension=0,
        tiled=True,
    )
    return (query_local[None], key_local[None], value_local[None], weight_grad)


def solution(mesh):
    placed = (
        P("dp", "ctx", None),
        P("dp", "ctx", None),
        P("dp", "ctx", None),
        P("dp", "ctx", None),
        P("dp", "ctx", None),
        P("dp", "ctx", None),
        P("dp", None),
        P("dp", None),
    )
    return jax.shard_map(
        local,
        mesh=mesh,
        in_specs=placed,
        out_specs=(
            P("dp", "ctx", None),
            P("dp", "ctx", None),
            P("dp", "ctx", None),
            P(("dp", "ctx"), None),
        ),
        check_vma=False,
    )
```

profile of v0, /device:TPU:1, one launch (start us, length us, event | category | flops | bytes accessed | tf_op | source)
XLA Modules:
  0.0 1757.2 jit_solution(17247154214299239792)
XLA Ops:
  17.3 43.6 %all-gather.2.cloned.1.call-done = bf16[8192,256]{1,0:T(8,128)(2,1)} async-done(((bf16[256,256]{1,0:T(8,128)(2,1)}), bf16[8192,256]{1,0:T(8,128)(2,1)}) %all-gather.2.cloned.1.call-update) | async-done | bytes 4194320 | tf_op jit(solution)/shard_map/all_gather | solution.py:141
  75.3 551.5 %while.44 = (s32[]{:T(128)}, f32[8192,256]{0,1:T(8,128)}, bf16[4,64,1024]{2,1,0:T(8,128)(2,1)}, s32[4,64]{1,0:T(4,128)S(1)}, s32[4]{0:T(128)S(1)}, /*index=5*/bf...) while((s32[]{:T(128)}, f32[8192,256]{0,1:T(8,128)}, ...), condition=%wide.region_18.19_spmd, body=%wide.region_4.18_spmd.sunk | while | flops 406785216 | bytes 15506935 | solution.py:120
  78.4 65.9 %while.45 = (s32[]{:T(128)}, f32[64,8]{1,0:T(8,128)S(1)}, f32[64,8]{1,0:T(8,128)}, s32[8192]{0:T(1024)}, s32[64]{0:T(128)S(1)}, /*index=5*/s32[64]{0:T(128)S(1)}...) while((s32[]{:T(128)}, f32[64,8]{1,0:T(8,128)S(1)}, ...), condition=%wide.region_12.12_spmd, body=%wide.region_6.11_spmd.sunk | while | flops 68814344 | bytes 3793759 | solution.py:66
  80.5 7.8 conditional.4
  146.1 66.3 %while.46 = (s32[]{:T(128)}, f32[512,128]{1,0:T(8,128)S(1)}, f32[8192,256]{0,1:T(8,128)}, s32[8192]{0:T(1024)}, s32[64]{0:T(128)S(1)}, /*index=5*/s32[64]{0:T(12...) while((s32[]{:T(128)}, f32[512,128]{1,0:T(8,128)S(1)}, ...), condition=%wide.region_17.17_spmd, body=%wide.region_13.16_spmd.sunk | while | flops 337838592 | bytes 9395087 | solution.py:109
  148.3 7.8 conditional.5
  158.3 7.8 conditional.5
  216.2 65.9 %while.45 = (s32[]{:T(128)}, f32[64,8]{1,0:T(8,128)S(1)}, f32[64,8]{1,0:T(8,128)}, s32[8192]{0:T(1024)}, s32[64]{0:T(128)S(1)}, /*index=5*/s32[64]{0:T(128)S(1)}...) while((s32[]{:T(128)}, f32[64,8]{1,0:T(8,128)S(1)}, ...), condition=%wide.region_12.12_spmd, body=%wide.region_6.11_spmd.sunk | while | flops 68814344 | bytes 3793759 | solution.py:66
  283.9 66.3 %while.46 = (s32[]{:T(128)}, f32[512,128]{1,0:T(8,128)S(1)}, f32[8192,256]{0,1:T(8,128)}, s32[8192]{0:T(1024)}, s32[64]{0:T(128)S(1)}, /*index=5*/s32[64]{0:T(12...) while((s32[]{:T(128)}, f32[512,128]{1,0:T(8,128)S(1)}, ...), condition=%wide.region_17.17_spmd, body=%wide.region_13.16_spmd.sunk | while | flops 337838592 | bytes 9395087 | solution.py:109
  286.1 7.8 conditional.5
  296.1 7.8 conditional.5
  354.1 65.9 %while.45 = (s32[]{:T(128)}, f32[64,8]{1,0:T(8,128)S(1)}, f32[64,8]{1,0:T(8,128)}, s32[8192]{0:T(1024)}, s32[64]{0:T(128)S(1)}, /*index=5*/s32[64]{0:T(128)S(1)}...) while((s32[]{:T(128)}, f32[64,8]{1,0:T(8,128)S(1)}, ...), condition=%wide.region_12.12_spmd, body=%wide.region_6.11_spmd.sunk | while | flops 68814344 | bytes 3793759 | solution.py:66
  421.8 66.3 %while.46 = (s32[]{:T(128)}, f32[512,128]{1,0:T(8,128)S(1)}, f32[8192,256]{0,1:T(8,128)}, s32[8192]{0:T(1024)}, s32[64]{0:T(128)S(1)}, /*index=5*/s32[64]{0:T(12...) while((s32[]{:T(128)}, f32[512,128]{1,0:T(8,128)S(1)}, ...), condition=%wide.region_17.17_spmd, body=%wide.region_13.16_spmd.sunk | while | flops 337838592 | bytes 9395087 | solution.py:109
  424.0 7.8 conditional.5
  434.0 7.8 conditional.5
  492.0 65.9 %while.45 = (s32[]{:T(128)}, f32[64,8]{1,0:T(8,128)S(1)}, f32[64,8]{1,0:T(8,128)}, s32[8192]{0:T(1024)}, s32[64]{0:T(128)S(1)}, /*index=5*/s32[64]{0:T(128)S(1)}...) while((s32[]{:T(128)}, f32[64,8]{1,0:T(8,128)S(1)}, ...), condition=%wide.region_12.12_spmd, body=%wide.region_6.11_spmd.sunk | while | flops 68814344 | bytes 3793759 | solution.py:66
  559.7 66.3 %while.46 = (s32[]{:T(128)}, f32[512,128]{1,0:T(8,128)S(1)}, f32[8192,256]{0,1:T(8,128)}, s32[8192]{0:T(1024)}, s32[64]{0:T(128)S(1)}, /*index=5*/s32[64]{0:T(12...) while((s32[]{:T(128)}, f32[512,128]{1,0:T(8,128)S(1)}, ...), condition=%wide.region_17.17_spmd, body=%wide.region_13.16_spmd.sunk | while | flops 337838592 | bytes 9395087 | solution.py:109
  561.9 7.8 conditional.5
  571.9 7.8 conditional.5
  626.8 9.0 copy.31
  651.1 400.9 %reduce-scatter.5.cloned.1.call-done = f32[256,256]{1,0:T(8,128)} async-done(((f32[8192,256]{1,0:T(8,128)}), f32[256,256]{1,0:T(8,128)}) %reduce-scatter.5.cloned.1.call-update) | async-done | bytes 262160 | tf_op jit(solution)/shard_map/reduce_scatter | solution.py:151
  1053.8 8.6 convolution_bitcast_fusion
  1062.4 22.5 %copy.34 = f32[4096,1280]{1,0:T(8,128)} copy(f32[4096,1280]{0,1:T(8,128)} %convolution_bitcast_fusion) | data formatting | bytes 41943040
  1087.1 663.5 %reduce-scatter.7.cloned.1.call-done = f32[32,1280]{1,0:T(8,128)} async-done(((f32[4096,1280]{1,0:T(8,128)}), f32[32,1280]{1,0:T(8,128)}) %reduce-scatter.7.cloned.1.call-update) | async-done | bytes 163856
  (1000 shorter events, 688.0 us)
Async XLA Ops:
  7.2 1046.6 %copy-start = (bf16[1,256,4096]{2,1,0:T(8,128)(2,1)S(1)}, bf16[1,256,4096]{2,1,0:T(8,128)(2,1)}, u32[]{:S(2)}) copy-start(bf16[1,256,4096]{2,1,0:T(8,128)(2,1)} %param.23) | copy-start | bytes 6291460
  7.2 8.7 copy-start.11
  7.2 53.7 %all-gather.2.cloned.1.call-start = ((), (), s32[]{:S(2)}) async-start(), calls=%async_computation.2 | async-start | bytes 4325376 | tf_op jit(solution)/shard_map/all_gather | solution.py:141
  8.9 1043.0 %reduce-scatter.5.cloned.1.call-start = ((), (), s32[]{:S(2)}) async-start(), calls=%async_computation.3 | async-start | bytes 8650752 | tf_op jit(solution)/shard_map/reduce_scatter | solution.py:151
  146.0 67.1 %copy-start.3 = (f32[4,64,8]{2,1,0:T(8,128)S(1)}, f32[4,64,8]{2,1,0:T(8,128)}, u32[]{:S(2)}) copy-start(f32[4,64,8]{2,1,0:T(8,128)} %copy-done.2) | copy-start | bytes 24580 | tf_op jit(solution)/shard_map/while
  146.0 67.1 %copy-start.8 = (s32[4,64]{1,0:T(4,128)S(1)}, s32[4,64]{1,0:T(4,128)}, u32[]{:S(2)}) copy-start(s32[4,64]{1,0:T(4,128)} %copy-done.7) | copy-start | bytes 3076 | tf_op jit(solution)/shard_map/while
  146.0 67.1 %copy-start.10 = (s32[4]{0:T(128)S(1)}, s32[4]{0:T(128)}, u32[]{:S(2)}) copy-start(s32[4]{0:T(128)} %copy-done.9) | copy-start | bytes 52 | tf_op jit(solution)/shard_map/while
  213.2 3.1 copy-start.2
  213.2 3.1 copy-start.7
  283.9 67.1 %copy-start.3 = (f32[4,64,8]{2,1,0:T(8,128)S(1)}, f32[4,64,8]{2,1,0:T(8,128)}, u32[]{:S(2)}) copy-start(f32[4,64,8]{2,1,0:T(8,128)} %copy-done.2) | copy-start | bytes 24580 | tf_op jit(solution)/shard_map/while
  283.9 67.1 %copy-start.8 = (s32[4,64]{1,0:T(4,128)S(1)}, s32[4,64]{1,0:T(4,128)}, u32[]{:S(2)}) copy-start(s32[4,64]{1,0:T(4,128)} %copy-done.7) | copy-start | bytes 3076 | tf_op jit(solution)/shard_map/while
  283.9 67.1 %copy-start.10 = (s32[4]{0:T(128)S(1)}, s32[4]{0:T(128)}, u32[]{:S(2)}) copy-start(s32[4]{0:T(128)} %copy-done.9) | copy-start | bytes 52 | tf_op jit(solution)/shard_map/while
  351.0 3.1 copy-start.2
  351.0 3.1 copy-start.7
  421.8 67.1 %copy-start.3 = (f32[4,64,8]{2,1,0:T(8,128)S(1)}, f32[4,64,8]{2,1,0:T(8,128)}, u32[]{:S(2)}) copy-start(f32[4,64,8]{2,1,0:T(8,128)} %copy-done.2) | copy-start | bytes 24580 | tf_op jit(solution)/shard_map/while
  421.8 67.1 %copy-start.8 = (s32[4,64]{1,0:T(4,128)S(1)}, s32[4,64]{1,0:T(4,128)}, u32[]{:S(2)}) copy-start(s32[4,64]{1,0:T(4,128)} %copy-done.7) | copy-start | bytes 3076 | tf_op jit(solution)/shard_map/while
  421.8 67.1 %copy-start.10 = (s32[4]{0:T(128)S(1)}, s32[4]{0:T(128)}, u32[]{:S(2)}) copy-start(s32[4]{0:T(128)} %copy-done.9) | copy-start | bytes 52 | tf_op jit(solution)/shard_map/while
  488.9 3.1 copy-start.2
  559.6 67.1 %copy-start.3 = (f32[4,64,8]{2,1,0:T(8,128)S(1)}, f32[4,64,8]{2,1,0:T(8,128)}, u32[]{:S(2)}) copy-start(f32[4,64,8]{2,1,0:T(8,128)} %copy-done.2) | copy-start | bytes 24580 | tf_op jit(solution)/shard_map/while
  559.6 67.1 %copy-start.8 = (s32[4,64]{1,0:T(4,128)S(1)}, s32[4,64]{1,0:T(4,128)}, u32[]{:S(2)}) copy-start(s32[4,64]{1,0:T(4,128)} %copy-done.7) | copy-start | bytes 3076 | tf_op jit(solution)/shard_map/while
  559.7 67.1 %copy-start.10 = (s32[4]{0:T(128)S(1)}, s32[4]{0:T(128)}, u32[]{:S(2)}) copy-start(s32[4]{0:T(128)} %copy-done.9) | copy-start | bytes 52 | tf_op jit(solution)/shard_map/while
  635.8 7.8 copy-start.6
  651.0 402.8 %copy-start.5 = (bf16[4,64,1024]{2,1,0:T(8,128)(2,1)S(1)}, bf16[4,64,1024]{2,1,0:T(8,128)(2,1)}, u32[]{:S(2)}) copy-start(bf16[4,64,1024]{2,1,0:T(8,128)(2,1)} %get-tuple-element.447) | copy-start | bytes 1572868
  651.0 1099.6 %reduce-scatter.7.cloned.1.call-start = ((), (), s32[]{:S(2)}) async-start(), calls=%async_computation.4 | async-start | bytes 21135360
  (24 other events, 32.0 us)
Sparse Core Ops, SparseCore 0:
  10.9 50.0 all-gather.1
  651.2 400.7 reduce-scatter.4
  1085.1 665.5 reduce-scatter.6
where the time goes:
time: 1790 us; the launch traced here: 1760 us
  waiting for transfers between devices  1110 us (62%)
  local copies, waits for them, and re-layouts  246 us (14%)
  other arithmetic  201 us (11%)
  matrix products  99.1 us (6%)
  loops' own time  88.4 us (5%)
    unnamed x4, waiting for transfers between devices  664 us
    reduce_scatter x1, waiting for transfers between devices, local(): lax.psum_scatter(device_grads, 'ctx', scatter_dimension=0, tiled=True)  401 us
    dynamic_slice x128, local copies, waits for them, and re-layouts, block_visible(): lax.dynamic_slice_in_dim(key_docs, block_index * key_block, key_block, 0)  97.8 us
    reduce_or x64, other arithmetic, stat_step(): return lax.cond(jnp.any(visible), stat_update, lambda kept: kept, carried)  47.3 us
    reduce_or x64, other arithmetic, grad_step(): return lax.cond(jnp.any(visible), grad_update, lambda kept: kept, carried)  47 us
    all_gather x1, waiting for transfers between devices, local(): gathered = lax.all_gather(stacked, 'ctx', axis=0, tiled=True)  43.6 us
    another operation x4, loops' own time, per_tile(): lax.fori_loop(0, block_count, grad_step, (start_query, kv_grads))  43.2 us
    another operation x4, loops' own time, per_tile(): running_max, summed = lax.fori_loop(0, block_count, stat_step, start_state)  41.3 us
  transfers between devices with their start and end apart: 3, of which 3 were waited for; matrix products, arithmetic and copies ran while one was open for 1% of the time, Pallas kernels for 0%

commit v1 on v0

v1 whole, which is shorter than its diff:
```python
import functools, math
import jax, jax.numpy as jnp
from jax import lax
from jax.experimental import pallas as pl
from jax.experimental.pallas import tpu as pltpu

F32 = jnp.float32
BF16 = jnp.bfloat16
NEG = -1e30


def dot(a, b):
    return jnp.dot(a, b, preferred_element_type=F32)


def attention_kernel(sets, heads, tok, dim, blocks,
                     ends_ref, held_ref, own_ref,
                     q_ref, do_ref, delta_ref, k_ref, v_ref,
                     dq_ref, dk_ref, dv_ref,
                     qt, dot_, kt, dqt, dka, dva, stat_m, stat_l, bias, seen):
    logit_scale = 1.0 / math.sqrt(dim)
    log2_scale = logit_scale * math.log2(math.e)

    dka[...] = jnp.zeros_like(dka)
    dva[...] = jnp.zeros_like(dva)
    for b in range(blocks):
        kt[b] = k_ref[b].T

    for rs in range(sets):
        own = own_ref[rs]
        span = held_ref[own]
        first = span * tok

        def count(d, lo):
            end = ends_ref[d]
            return jnp.where(end <= first, jnp.maximum(lo, end), lo)

        doc_count = ends_ref.shape[0]
        lo_first = lax.fori_loop(0, doc_count, count, jnp.int32(0))
        seen[0] = own

        def collect(b, n):
            h = held_ref[b]
            take = (h < span) & (h * tok + (tok - 1) >= lo_first)

            @pl.when(take)
            def _():
                seen[n] = b

            return n + take.astype(jnp.int32)

        total = lax.fori_loop(0, blocks, collect, jnp.int32(1))
        for h in range(heads):
            rows = pl.ds(h * dim, dim)
            qt[rows, :] = q_ref[rs, :, rows].T
            dot_[rows, :] = do_ref[rs, :, rows].T
        pos = first + lax.broadcasted_iota(jnp.int32, (1, tok), 1)
        low = jnp.zeros((1, tok), jnp.int32)
        for d in range(doc_count):
            end = ends_ref[d]
            low = jnp.where(pos >= end, jnp.maximum(low, end), low)

        stat_m[...] = jnp.full_like(stat_m, NEG)
        stat_l[...] = jnp.zeros_like(stat_l)
        dqt[...] = jnp.zeros_like(dqt)

        def set_bias(b):
            kp = held_ref[b] * tok + lax.broadcasted_iota(jnp.int32, (tok, tok), 0)
            bias[...] = jnp.where((kp >= low) & (kp <= pos), 0.0, NEG)

        def pass_one(i, carry):
            b = seen[i]
            set_bias(b)
            k = k_ref[b]
            for h in range(heads):
                s = dot(k, qt[pl.ds(h * dim, dim), :]) * log2_scale + bias[...]
                m_old = stat_m[pl.ds(h, 1), :]
                m_new = jnp.maximum(m_old, jnp.max(s, axis=0, keepdims=True))
                add = jnp.sum(jnp.exp2(s - m_new), axis=0, keepdims=True)
                stat_l[pl.ds(h, 1), :] = stat_l[pl.ds(h, 1), :] * jnp.exp2(m_old - m_new) + add
                stat_m[pl.ds(h, 1), :] = m_new
            return carry

        lax.fori_loop(0, total, pass_one, 0)
        stat_m[...] = stat_m[...] + jnp.log2(stat_l[...])

        def pass_two(i, carry):
            b = seen[i]
            set_bias(b)
            k = k_ref[b]
            v = v_ref[b]
            ktb = kt[b]
            dk = dka[b]
            dv = dva[b]
            for h in range(heads):
                rows = pl.ds(h * dim, dim)
                s = dot(k, qt[rows, :]) * log2_scale + bias[...]
                p = jnp.exp2(s - stat_m[pl.ds(h, 1), :])
                dp = dot(v, dot_[rows, :])
                ds = (p * (dp - delta_ref[rs, pl.ds(h, 1), :])).astype(BF16)
                dv = dv + dot(p.astype(BF16), do_ref[rs, :, rows])
                dk = dk + dot(ds, q_ref[rs, :, rows])
                dqt[rows, :] += dot(ktb, ds)
            dka[b] = dk
            dva[b] = dv
            return carry

        lax.fori_loop(0, total, pass_two, 0)
        for h in range(heads):
            rows = pl.ds(h * dim, dim)
            dq_ref[rs, :, rows] = (logit_scale * dqt[rows, :]).T.astype(BF16)

    def write(b, carry):
        dk_ref[b] = dka[b].astype(dk_ref.dtype)
        dv_ref[b] = dva[b].astype(dv_ref.dtype)
        return carry

    lax.fori_loop(0, blocks, write, 0)


def attention(ends, held, own, q, do, delta, k, v, out_dtype=BF16):
    sets, tok, width = q.shape
    blocks, _, dim = k.shape
    heads = width // dim
    smem = pl.BlockSpec(memory_space=pltpu.SMEM)
    vmem = pl.BlockSpec(memory_space=pltpu.VMEM)
    return pl.pallas_call(
        functools.partial(attention_kernel, sets, heads, tok, dim, blocks),
        out_shape=(
            jax.ShapeDtypeStruct(q.shape, BF16),
            jax.ShapeDtypeStruct(k.shape, out_dtype),
            jax.ShapeDtypeStruct(k.shape, out_dtype),
        ),
        in_specs=[smem, smem, smem, vmem, vmem, vmem, vmem, vmem],
        out_specs=(vmem, vmem, vmem),
        scratch_shapes=[
            pltpu.VMEM((width, tok), BF16),
            pltpu.VMEM((width, tok), BF16),
            pltpu.VMEM((blocks, dim, tok), BF16),
            pltpu.VMEM((width, tok), F32),
            pltpu.VMEM((blocks, tok, dim), F32),
            pltpu.VMEM((blocks, tok, dim), F32),
            pltpu.VMEM((heads, tok), F32),
            pltpu.VMEM((heads, tok), F32),
            pltpu.VMEM((tok, tok), F32),
            pltpu.SMEM((blocks + 1,), jnp.int32),
        ],
        compiler_params=pltpu.CompilerParams(vmem_limit_bytes=56 * 2**20),
        name="attention",
    )(ends, held, own, q, do, delta, k, v)


def local(
    queries, key_rows, value_rows, forward_out, out_grad, layer_input, doc_lengths, held_span
):
    tok = queries.shape[1]
    dim = key_rows.shape[2]
    heads = queries.shape[2] // dim
    scale = 1.0 / math.sqrt(dim)
    ctx = lax.axis_size("ctx")
    me = lax.axis_index("ctx").astype(jnp.int32)
    ends = jnp.cumsum(doc_lengths[0]).astype(jnp.int32)
    held = held_span[0]
    stacked = jnp.stack([key_rows[0], value_rows[0]])
    both = lax.all_gather(stacked, "ctx", axis=0)
    k, v = both[:, 0], both[:, 1]
    delta = jnp.sum(
        (out_grad[0].astype(F32) * forward_out[0].astype(F32)).reshape(tok, heads, dim), axis=2
    ).T[None]
    dq, dk, dv = attention(ends, held, me[None], queries, out_grad, delta, k, v, F32)
    grads = jnp.concatenate([dk, dv], axis=2).reshape(ctx * tok, 2 * dim)
    own = lax.psum_scatter(grads, "ctx", scatter_dimension=0, tiled=True)
    key_local = (scale * own[:, :dim]).astype(BF16)
    value_local = own[:, dim:].astype(BF16)
    joined = jnp.concatenate([dq[0], key_local, value_local], axis=1)
    weight = lax.psum_scatter(
        lax.dot_general(layer_input[0], joined, (((0,), (0,)), ((), ())), preferred_element_type=F32),
        ("dp", "ctx"), scatter_dimension=0, tiled=True,
    )
    return dq, key_local[None], value_local[None], weight


def solution(mesh):
    from jax.sharding import PartitionSpec as P
    row = P("dp", "ctx", None)
    flat = P("dp", None)
    return jax.shard_map(
        local, mesh=mesh, in_specs=(row,) * 6 + (flat,) * 2,
        out_specs=(row, row, row, P(("dp", "ctx"), None)), check_vma=False,
    )
```

time: 1790 us -> 933 us (0.52); the launches traced: 1760 us -> 926 us
  waiting for transfers between devices: 1110 us -> 840 us
  local copies, waits for them, and re-layouts: 246 us -> 30.6 us
  other arithmetic: 201 us -> 13 us
  matrix products: 99.1 us -> 8.59 us
  loops' own time: 88.4 us -> 0 us
  Pallas kernels: 0 us -> 20 us
    reduce_scatter x1, waiting for transfers between devices: 401 us -> 126 us  [local(): own = lax.psum_scatter(grads, 'ctx', scatter_dimension=0, tiled=True)]
    dynamic_slice x132 -> x0, local copies, waits for them, and re-layouts: 104 us -> none  [the longest x128 97.8 us: block_visible(): lax.dynamic_slice_in_dim(key_docs, block_index * key_block, key_block, 0)]
    reduce_or x128 -> x0, other arithmetic: 94.3 us -> none  [the longest x64 47.3 us: stat_step(): return lax.cond(jnp.any(visible), stat_update, lambda kept: kept, carried)]
    dot_general x97 -> x1, matrix products: 99.1 us -> 8.59 us  [local(): lax.dot_general(layer_input[0], joined, (((0,), (0,)), ((), ())), preferr...]
    another operation x137 -> x0, loops' own time: 88.4 us -> none  [the longest x4 43.2 us: per_tile(): lax.fori_loop(0, block_count, grad_step, (start_query, kv_grads))]
    dynamic_update_slice x16 -> x0, other arithmetic: 31 us -> none  [grad_update(): lax.dynamic_update_slice_in_dim(kv_acc, previous + jnp.concatenate([key_t...]
    sub x48 -> x0, local copies, waits for them, and re-layouts: 28.5 us -> none  [the longest x16 13.6 us: grad_update(): logit_grad = probs * (prob_grad - tile_delta[:, :, None])]
    add x149 -> x0, other arithmetic: 26.9 us -> none  [the longest x16 22.8 us: stat_update(): summed * jnp.exp(running_max - new_max) + jnp.sum(terms, axis=2)]
  transfers between devices with their start and end apart: 3 -> 3, of which waited for: 3 -> 3; matrix products, arithmetic and copies ran while one was open for 1% -> 0% of each run, Pallas kernels for 0% -> 0%
where the time goes in v1:
time: 933 us; the launch traced here: 926 us
  waiting for transfers between devices  840 us (90%)
  local copies, waits for them, and re-layouts  30.6 us (3%)
  Pallas kernels  20 us (2%)
  between operations  13.8 us (1%)
  other arithmetic  13 us (1%)
    unnamed x4, waiting for transfers between devices  665 us
    reduce_scatter x1, waiting for transfers between devices, local(): own = lax.psum_scatter(grads, 'ctx', scatter_dimension=0, tiled=True)  126 us
    all_gather x1, waiting for transfers between devices, local(): both = lax.all_gather(stacked, 'ctx', axis=0)  48.6 us
    unnamed x12, local copies, waits for them, and re-layouts  23.7 us
    pallas_call x1, Pallas kernels, attention(): pl.pallas_call(functools.partial(attention_kernel, sets, heads, tok, dim,...  20 us
  transfers between devices with their start and end apart: 3, of which 3 were waited for; matrix products, arithmetic and copies ran while one was open for 0% of the time, Pallas kernels for 0%

profile of v1, /device:TPU:1, one launch (start us, length us, event | category | flops | bytes accessed | tf_op | source)
XLA Modules:
  0.0 926.3 jit_solution(79426879073665035)
XLA Ops:
  7.2 0.0 all-gather.3.cloned.1.call-start
  7.2 1.7 pad_maximum_fusion.1
  8.9 0.0 all-gather.3.cloned.1.call-update
  8.9 0.0 reduce-scatter.5.cloned.1.call-start
  9.0 1.4 multiply_bitcast_fusion
  10.4 0.2 copy.24
  10.6 0.3 reduce_sum.9
  10.9 0.7 copy.16
  11.6 0.7 reduce-window.9
  12.3 48.6 %all-gather.3.cloned.1.call-done = bf16[64,256,128]{2,1,0:T(8,128)(2,1)} async-done(((bf16[2,256,128]{2,1,0:T(8,128)(2,1)}), bf16[64,256,128]{2,1,0:T(8,128)(2,1)}) %all-gather.3.cloned.1.call-update) | async-done | bytes 4194320 | tf_op jit(solution)/shard_map/all_gather | solution.py:165
  60.9 4.7 slice_bitcast_fusion
  65.6 20.0 %attention.1 = (bf16[1,256,1024]{2,1,0:T(8,128)(2,1)}, f32[32,256,128]{2,1,0:T(8,128)}, f32[32,256,128]{2,1,0:T(8,128)}) custom-call(s32[4]{0:T(128)} %bitcast.38, s32[32]{0:T(128)} %bitcast.37, s32[1]{0:T(128)} %bitcast.3.own_ref, bf16[1,256,1024]{2,1,0:T(8,128)(2,1)} %q_ref.1, bf16[1,256,1024]{2,1,0:T(8,128)(2,1)} %do_ref.1, f32[1,8,256]{2,1,0:T(8,128)} %bitcast.36, ...), custom_call_target="tpu_custom_call" | custom-call | tf_op jit(solution)/shard_map/attention/pallas_call | solution.py:127
  85.6 7.3 pad_maximum_fusion
  93.0 0.0 reduce-scatter.7.cloned.1.call-start
  93.1 126.2 %reduce-scatter.5.cloned.1.call-done = f32[256,256]{1,0:T(8,128)} async-done(((f32[8192,256]{1,0:T(8,128)}), f32[256,256]{1,0:T(8,128)}) %reduce-scatter.5.cloned.1.call-update) | async-done | bytes 262160 | tf_op jit(solution)/shard_map/reduce_scatter | solution.py:172
  219.2 0.9 slice.27
  220.1 0.9 fusion.6
  221.1 8.6 convolution_bitcast_fusion
  229.7 22.5 %copy.20 = f32[4096,1280]{1,0:T(8,128)} copy(f32[4096,1280]{0,1:T(8,128)} %convolution_bitcast_fusion) | data formatting | bytes 41943040
  252.2 0.0 reduce-scatter.7.cloned.1.call-update
  252.2 0.9 copy-done.2
  253.1 0.6 fusion.8
  253.8 0.6 slice_bitcast_fusion.2
  254.4 665.3 %reduce-scatter.7.cloned.1.call-done = f32[32,1280]{1,0:T(8,128)} async-done(((f32[4096,1280]{1,0:T(8,128)}), f32[32,1280]{1,0:T(8,128)}) %reduce-scatter.7.cloned.1.call-update) | async-done | bytes 163856
  (10 shorter events, 0.0 us)
Async XLA Ops:
  7.2 213.9 %copy-start = (bf16[1,256,4096]{2,1,0:T(8,128)(2,1)S(1)}, bf16[1,256,4096]{2,1,0:T(8,128)(2,1)}, u32[]{:S(2)}) copy-start(bf16[1,256,4096]{2,1,0:T(8,128)(2,1)} %param.13) | copy-start | bytes 6291460
  7.2 4.4 copy-start.4
  7.2 53.7 %all-gather.3.cloned.1.call-start = ((), (), s32[]{:S(2)}) async-start(), calls=%async_computation.3 | async-start | bytes 4325376 | tf_op jit(solution)/shard_map/all_gather | solution.py:165
  8.9 210.3 %reduce-scatter.5.cloned.1.call-start = ((), (), s32[]{:S(2)}) async-start(), calls=%async_computation.2 | async-start | bytes 8650752 | tf_op jit(solution)/shard_map/reduce_scatter | solution.py:172
  93.0 128.1 %copy-start.3 = (bf16[1,256,1024]{2,1,0:T(8,128)(2,1)S(1)}, bf16[1,256,1024]{2,1,0:T(8,128)(2,1)}, u32[]{:S(2)}) copy-start(bf16[1,256,1024]{2,1,0:T(8,128)(2,1)} %get-tuple-element.18) | copy-start | bytes 1572868
  93.0 826.8 %reduce-scatter.7.cloned.1.call-start = ((), (), s32[]{:S(2)}) async-start(), calls=%async_computation.4 | async-start | bytes 21135360
  252.2 0.9 copy-start.2
  253.1 666.6 %copy-start.1 = (bf16[1,256,4096]{2,1,0:T(8,128)(2,1)S(1)}, bf16[1,256,4096]{2,1,0:T(8,128)(2,1)}, u32[]{:S(2)}) copy-start(bf16[1,256,4096]{2,1,0:T(8,128)(2,1)} %param.13) | copy-start | bytes 6291460
Sparse Core Ops, SparseCore 0:
  10.9 50.0 all-gather.2
  93.1 126.0 reduce-scatter.4
  252.3 667.3 reduce-scatter.6

commit v2 on v1

--- a/solution.py
+++ b/solution.py
@@ -3,9 +3,11 @@
 from jax import lax
 from jax.experimental import pallas as pl
 from jax.experimental.pallas import tpu as pltpu
+from jax.sharding import PartitionSpec as P
 
 F32 = jnp.float32
 BF16 = jnp.bfloat16
+MESH = pl.DeviceIdType.MESH
 NEG = -1e30
 
 
@@ -16,16 +18,13 @@
 def attention_kernel(sets, heads, tok, dim, blocks,
                      ends_ref, held_ref, own_ref,
                      q_ref, do_ref, delta_ref, k_ref, v_ref,
-                     dq_ref, dk_ref, dv_ref,
+                     dq_ref, dkv_ref,
                      qt, dot_, kt, dqt, dka, dva, stat_m, stat_l, bias, seen):
     logit_scale = 1.0 / math.sqrt(dim)
     log2_scale = logit_scale * math.log2(math.e)
 
     dka[...] = jnp.zeros_like(dka)
     dva[...] = jnp.zeros_like(dva)
-    for b in range(blocks):
-        kt[b] = k_ref[b].T
-
     for rs in range(sets):
         own = own_ref[rs]
         span = held_ref[own]
@@ -72,6 +71,7 @@
             b = seen[i]
             set_bias(b)
             k = k_ref[b]
+            kt[b] = k.T
             for h in range(heads):
                 s = dot(k, qt[pl.ds(h * dim, dim), :]) * log2_scale + bias[...]
                 m_old = stat_m[pl.ds(h, 1), :]
@@ -111,14 +111,14 @@
             dq_ref[rs, :, rows] = (logit_scale * dqt[rows, :]).T.astype(BF16)
 
     def write(b, carry):
-        dk_ref[b] = dka[b].astype(dk_ref.dtype)
-        dv_ref[b] = dva[b].astype(dv_ref.dtype)
+        dkv_ref[0, b] = dka[b].astype(BF16)
+        dkv_ref[1, b] = dva[b].astype(BF16)
         return carry
 
     lax.fori_loop(0, blocks, write, 0)
 
 
-def attention(ends, held, own, q, do, delta, k, v, out_dtype=BF16):
+def attention(ends, held, own, q, do, delta, k, v):
     sets, tok, width = q.shape
     blocks, _, dim = k.shape
     heads = width // dim
@@ -128,11 +128,10 @@
         functools.partial(attention_kernel, sets, heads, tok, dim, blocks),
         out_shape=(
             jax.ShapeDtypeStruct(q.shape, BF16),
-            jax.ShapeDtypeStruct(k.shape, out_dtype),
-            jax.ShapeDtypeStruct(k.shape, out_dtype),
+            jax.ShapeDtypeStruct((2,) + k.shape, BF16),
         ),
         in_specs=[smem, smem, smem, vmem, vmem, vmem, vmem, vmem],
-        out_specs=(vmem, vmem, vmem),
+        out_specs=(vmem, vmem),
         scratch_shapes=[
             pltpu.VMEM((width, tok), BF16),
             pltpu.VMEM((width, tok), BF16),
@@ -150,38 +149,482 @@
     )(ends, held, own, q, do, delta, k, v)
 
 
+def split_axis(t):
+    return t // 2, lax.rem(t + t // 2, 2)
+
+
+class Place:
+    def __init__(self, with_dp):
+        y = lax.axis_index("dp")
+        me = lax.axis_index("ctx")
+        z, x, c = me // 8, lax.rem(me // 2, 4), lax.rem(me, 2)
+        self.core = c
+        self.sibling = {"dp": y, "ctx": me + 1 - 2 * c}
+
+        def at(y, z, x):
+            return {"dp": y, "ctx": z * 8 + x * 2 + c}
+
+        def low(t):
+            return t + 1 - 2 * lax.rem(t, 2)
+
+        self.bits = split_axis(z) + split_axis(x)
+        self.partners = (at(y, 3 - z, x), at(y, low(z), x), at(y, z, 3 - x), at(y, z, low(x)))
+        if with_dp:
+            self.bits = split_axis(y) + self.bits
+            self.partners = (at(3 - y, z, x), at(low(y), z, x)) + self.partners
+        self.dims = len(self.bits)
+
+    def greet(self):
+        barrier = pltpu.get_barrier_semaphore()
+        everyone = (self.sibling,) + self.partners
+        for other in everyone:
+            pl.semaphore_signal(barrier, inc=1, device_id=other, device_id_type=MESH)
+        pl.semaphore_wait(barrier, len(everyone))
+
+    def spot(self, free, flipped=None):
+        found = []
+        for d in range(self.dims):
+            if d in free:
+                found.append(slice(None))
+            elif d == flipped:
+                found.append(1 - self.bits[d])
+            else:
+                found.append(self.bits[d])
+        return tuple(found)
+
+
+def remote(src, dst, send, recv, to):
+    return pltpu.make_async_remote_copy(
+        src_ref=src, dst_ref=dst, send_sem=send, recv_sem=recv, device_id=to, device_id_type=MESH
+    )
+
+
+def turns(dims, start):
+    return [(start + s) % dims for s in range(dims)]
+
+
+def gather_kernel(k_ref, v_ref, q_ref, do_ref, o_ref, x_ref,
+                  k_all, v_all, q_two, do_two, delta_two, xt_two,
+                  x_buf, do_buf, o_buf, xt_buf, delta_buf,
+                  hop_send, hop_recv, pass_send, pass_recv, side_send, side_recv, local_sem):
+    tok, dim = k_ref.shape
+    half = q_two.shape[2]
+    here = Place(False)
+    c = here.core
+    dims = here.dims
+    quarter = tok // dims
+    sources, targets = (k_ref, v_ref), (k_all, v_all)
+
+    loads = [
+        pltpu.make_async_copy(do_ref, do_buf, local_sem.at[0]),
+        pltpu.make_async_copy(o_ref, o_buf, local_sem.at[1]),
+        pltpu.make_async_copy(x_ref, x_buf, local_sem.at[2]),
+    ]
+    keeps = [
+        pltpu.make_async_copy(k_ref, k_all.at[here.bits + (c,)], local_sem.at[3]),
+        pltpu.make_async_copy(v_ref, v_all.at[here.bits + (c,)], local_sem.at[4]),
+        pltpu.make_async_copy(q_ref.at[:, pl.ds(c * half, half)], q_two.at[c], local_sem.at[5]),
+        pltpu.make_async_copy(do_ref.at[:, pl.ds(c * half, half)], do_two.at[c], local_sem.at[6]),
+    ]
+    for copy in loads + keeps:
+        copy.start()
+    here.greet()
+
+    def rows(p):
+        return (pl.ds(p * quarter, quarter), slice(None))
+
+    hops = {}
+    for p in range(dims):
+        for kind in range(2):
+            n = (p * dims) * 2 + kind
+            hops[p, 0, kind] = remote(
+                sources[kind].at[rows(p)],
+                targets[kind].at[here.bits + (c,) + rows(p)],
+                hop_send.at[n], hop_recv.at[n], here.partners[turns(dims, p)[0]],
+            )
+            hops[p, 0, kind].start()
+    sides = []
+    to_side = [
+        (k_ref, k_all.at[here.bits + (c,)]),
+        (v_ref, v_all.at[here.bits + (c,)]),
+        (q_ref.at[:, pl.ds((1 - c) * half, half)], q_two.at[c]),
+        (do_ref.at[:, pl.ds((1 - c) * half, half)], do_two.at[c]),
+    ]
+
+    def aside(src, dst):
+        n = len(sides)
+        sides.append(remote(src, dst, side_send.at[n], side_recv.at[n], here.sibling))
+        sides[-1].start()
+
+    for src, dst in to_side:
+        aside(src, dst)
+
+    passes = []
+
+    def hand_on(p, s):
+        order = turns(dims, p)
+        for kind in range(2):
+            n = (p * dims + s) * 2 + kind
+            hops[p, s, kind].wait_recv()
+            part = targets[kind].at[here.spot(order[:s], order[s]) + (c,) + rows(p)]
+            copy = remote(part, part, pass_send.at[n], pass_recv.at[n], here.sibling)
+            copy.start()
+            passes.append(copy)
+
+    def hop(p, s):
+        order = turns(dims, p)
+        for kind in range(2):
+            n = (p * dims + s) * 2 + kind
+            part = targets[kind].at[here.spot(order[:s]) + (c,) + rows(p)]
+            hops[p, s, kind] = remote(
+                part, part, hop_send.at[n], hop_recv.at[n], here.partners[order[s]]
+            )
+            hops[p, s, kind].start()
+
+    for copy in keeps:
+        copy.wait()
+
+    loads[0].wait()
+    loads[1].wait()
+    heads = half // dim
+    for h in range(2 * heads):
+        cols = pl.ds(h * dim, dim)
+        products = do_buf[:, cols].astype(F32) * o_buf[:, cols].astype(F32)
+        delta_buf[h // heads, pl.ds(h % heads, 1), :] = jnp.sum(products.T, axis=0, keepdims=True)
+    for h in range(heads, delta_buf.shape[1]):
+        delta_buf[:, pl.ds(h, 1), :] = jnp.zeros((2, 1, tok), F32)
+    own_delta = pltpu.make_async_copy(delta_buf.at[c], delta_two.at[c], local_sem.at[7])
+    own_delta.start()
+    aside(delta_buf.at[1 - c], delta_two.at[c])
+
+    for p in range(dims):
+        hand_on(p, 0)
+        hop(p, 1)
+    loads[2].wait()
+
+    def turn(i, carry):
+        xt_buf[pl.ds(i * 128, 128), :] = x_buf[:, pl.ds(i * 128, 128)].T
+        return carry
+
+    steps = x_ref.shape[1] // 128
+    lax.fori_loop(0, steps // 2, turn, 0)
+    for p in range(dims):
+        hand_on(p, 1)
+        hop(p, 2)
+    lax.fori_loop(steps // 2, steps, turn, 0)
+    mine = xt_two.at[:, pl.ds(c * tok, tok)]
+    own_xt = pltpu.make_async_copy(xt_buf, mine, local_sem.at[8])
+    own_xt.start()
+    for p in range(dims):
+        hand_on(p, 2)
+        hop(p, 3)
+    aside(xt_buf, mine)
+    for p in range(dims):
+        hand_on(p, 3)
+    own_delta.wait()
+    own_xt.wait()
+    for copy in hops.values():
+        copy.wait_send()
+    for copy in passes:
+        copy.wait()
+    for copy in sides:
+        copy.wait()
+
+
+def gather(k, v, q, do, o, x):
+    tok, dim = k.shape
+    half = q.shape[1] // 2
+    anywhere = pl.BlockSpec(memory_space=pl.ANY)
+    dma = pltpu.SemaphoreType.DMA
+    full = jax.ShapeDtypeStruct((2, 2, 2, 2, 2, tok, dim), BF16)
+    return pl.pallas_call(
+        gather_kernel,
+        out_shape=(
+            full, full,
+            jax.ShapeDtypeStruct((2, tok, half), BF16),
+            jax.ShapeDtypeStruct((2, tok, half), BF16),
+            jax.ShapeDtypeStruct((2, 8, tok), F32),
+            jax.ShapeDtypeStruct((x.shape[1], 2 * tok), BF16),
+        ),
+        in_specs=[anywhere] * 6,
+        out_specs=(anywhere,) * 6,
+        scratch_shapes=[
+            pltpu.VMEM(x.shape, BF16),
+            pltpu.VMEM(q.shape, BF16),
+            pltpu.VMEM(q.shape, BF16),
+            pltpu.VMEM((x.shape[1], tok), BF16),
+            pltpu.VMEM((2, 8, tok), F32),
+            dma((32,)), dma((32,)), dma((32,)), dma((32,)), dma((6,)), dma((6,)), dma((9,)),
+        ],
+        compiler_params=pltpu.CompilerParams(
+            collective_id=1, has_side_effects=True, vmem_limit_bytes=40 * 2**20
+        ),
+        name="gather",
+    )(k, v, q, do, o, x)
+
+
+def wide_parts(rows, cols):
+    cut = cols // 4 * 3
+    quarter, half = rows // 4, rows // 2
+    return [(i * quarter, quarter, 0, cut) for i in range(4)] + [
+        (i * half, half, cut, cols - cut) for i in range(2)
+    ]
+
+
+def thin_parts(rows, cols):
+    return [(i * (rows // 4), rows // 4, 0, cols) for i in range(4)]
+
+
+class Halving:
+    def __init__(self, here, acc, parts, orders, landing, send, recv):
+        self.here, self.acc, self.parts, self.orders = here, acc, parts, orders
+        self.landing, self.send_sem, self.recv_sem = landing, send, recv
+        self.copies = {}
+
+    def index(self, p, s, flip):
+        r0, nr, c0, nc = self.parts[p]
+        order = self.orders[p]
+        free = order[s + 1:]
+        d = order[s]
+        return self.here.spot(free, d if flip else None) + self.cut(r0, nr, c0, nc)
+
+    def cut(self, r0, nr, c0, nc):
+        return (slice(None),) * (len(self.acc.shape) - self.here.dims - 2) + (
+            pl.ds(r0, nr), pl.ds(c0, nc))
+
+    def send(self, p, s):
+        dims = self.here.dims
+        n = p * dims + s
+        copy = remote(
+            self.acc.at[self.index(p, s, True)], self.landing[n],
+            self.send_sem.at[n], self.recv_sem.at[n], self.here.partners[self.orders[p][s]],
+        )
+        copy.start()
+        self.copies[p, s] = copy
+
+    def total(self, p, s):
+        self.copies[p, s].wait_recv()
+        n = p * self.here.dims + s
+        return self.acc[self.index(p, s, False)].astype(F32) + self.landing[n][...].astype(F32)
+
+    def add(self, p, s):
+        self.acc[self.index(p, s, False)] = self.total(p, s).astype(self.acc.dtype)
+
+    def finish(self):
+        for copy in self.copies.values():
+            copy.wait_send()
+
+
+def landing_shapes(parts, orders, extra):
+    shapes = []
+    for (_, nr, _, nc), order in zip(parts, orders):
+        for s in range(len(order)):
+            shapes.append((2,) * (len(order) - 1 - s) + extra + (nr, nc))
+    return shapes
+
+
+def layout(tok, dim, half, features):
+    row_chunk = features // 64
+    kv_parts = thin_parts(tok, dim)
+    kv_orders = [turns(4, p) for p in range(4)]
+    wide = wide_parts(row_chunk, half)
+    wide_orders = [turns(6, p) for p in range(6)]
+    thin = thin_parts(row_chunk, dim)
+    thin_orders = [turns(6, p) for p in (0, 2, 3, 5)]
+    return row_chunk, kv_parts, kv_orders, wide, wide_orders, thin, thin_orders
+
+
+def reduce_kernel(plan, scale, dkv_ref, dq_ref, xt_ref, qg_ref, kvg_ref, wg_ref, *scratch):
+    row_chunk, kv_parts, kv_orders, wide, wide_orders, thin, thin_orders = plan
+    (kv_acc, kv_in, kv_mine, w_acc, t_acc, xt, dq, fin, kv_send, kv_recv, w_send, w_recv, t_send, t_recv,
+     side_send, side_recv, local_sem) = scratch[:17]
+    landing = scratch[17:]
+    tok, dim = dkv_ref.shape[-2:]
+    half = dq_ref.shape[2]
+    here_w = Place(True)
+    here = Place(False)
+    c = here.core
+    n_kv, n_w = 16, 36
+    kv = Halving(here, kv_acc, kv_parts, kv_orders, landing[:n_kv], kv_send, kv_recv)
+    w = Halving(here_w, w_acc, wide, wide_orders, landing[n_kv:n_kv + n_w], w_send, w_recv)
+    t = Halving(here_w, t_acc, thin, thin_orders, landing[n_kv + n_w:], t_send, t_recv)
+
+    loads = [
+        pltpu.make_async_copy(dq_ref, dq, local_sem.at[0]),
+        pltpu.make_async_copy(xt_ref, xt, local_sem.at[1]),
+        pltpu.make_async_copy(dkv_ref.at[c], kv_acc, local_sem.at[2]),
+        pltpu.make_async_copy(dq_ref.at[c], qg_ref.at[:, pl.ds(c * half, half)], local_sem.at[3]),
+    ]
+    for copy in loads:
+        copy.start()
+    here_w.greet()
+    sides = []
+
+    def aside(src, dst):
+        n = len(sides)
+        sides.append(remote(src, dst, side_send.at[n], side_recv.at[n], here.sibling))
+        sides[-1].start()
+
+    rest = (slice(None),) * 5
+    for p in range(4):
+        r0, nr, _, _ = kv_parts[p]
+        aside(dkv_ref.at[(1 - c,) + rest + (pl.ds(r0, nr),)], kv_in.at[rest + (pl.ds(r0, nr),)])
+    aside(dq_ref.at[1 - c], qg_ref.at[:, pl.ds(c * half, half)])
+
+    loads[2].wait()
+    for p in range(4):
+        r0, nr, _, _ = kv_parts[p]
+        sides[p].wait_recv()
+
+        def join(i, carry, r0=r0, nr=nr):
+            at = (i // 8, lax.rem(i // 4, 2), lax.rem(i // 2, 2), lax.rem(i, 2), slice(None), pl.ds(r0, nr))
+            kv_acc[at] = (kv_acc[at].astype(F32) + kv_in[at].astype(F32)).astype(BF16)
+            return carry
+
+        lax.fori_loop(0, 16, join, 0)
+        kv.send(p, 0)
+
+    loads[0].wait()
+    loads[1].wait()
+
+    def products(i, right, acc):
+        block = dot(xt[pl.ds(i * 8 * row_chunk, 8 * row_chunk), :], right).astype(BF16)
+        y = i // 2
+        for j in range(8):
+            z = 2 * lax.rem(i, 2) + j // 4
+            x = j % 4
+            at = split_axis(y) + split_axis(z) + (x // 2, (x + x // 2) % 2)
+            acc[at] = block[j * row_chunk:(j + 1) * row_chunk]
+
+    both = dq[...].reshape(2 * tok, half)
+
+    def wide_products(i, carry):
+        products(i, both, w_acc)
+        return carry
+
+    lax.fori_loop(0, 8, wide_products, 0)
+    for p in range(6):
+        w.send(p, 0)
+    for s in range(1, 4):
+        for p in range(4):
+            kv.add(p, s - 1)
+            kv.send(p, s)
+    kv_scale = jnp.where(c == 0, scale, 1.0).astype(F32)
+    for p in range(4):
+        r0, nr, _, _ = kv_parts[p]
+        kv_mine[:, pl.ds(r0, nr), :] = (kv.total(p, 3) * kv_scale).astype(BF16)
+    own_kv = pltpu.make_async_copy(kv_mine.at[c], kvg_ref.at[c], local_sem.at[4])
+    own_kv.start()
+    aside(kv_mine.at[1 - c], kvg_ref.at[c])
+    mine = kv_mine[...].reshape(2 * tok, dim)
+
+    def thin_products(i, carry):
+        products(i, mine, t_acc)
+        return carry
+
+    lax.fori_loop(0, 8, thin_products, 0)
+    for p in range(4):
+        t.send(p, 0)
+    for s in range(1, 6):
+        for p in range(6):
+            w.add(p, s - 1)
+            w.send(p, s)
+        for p in range(4):
+            t.add(p, s - 1)
+            t.send(p, s)
+    for p, (r0, nr, c0, nc) in enumerate(wide):
+        fin[pl.ds(r0, nr), pl.ds(c0, nc)] = w.total(p, 5)
+    for p, (r0, nr, c0, nc) in enumerate(thin):
+        fin[pl.ds(r0, nr), pl.ds(half, nc)] = t.total(p, 5)
+    rows_out = row_chunk // 2
+    pieces = [(0, c * half, half), (half, 2 * half + c * dim, dim)]
+    own_w = []
+    for n, (src, dst, width) in enumerate(pieces):
+        own_w.append(pltpu.make_async_copy(
+            fin.at[pl.ds(c * rows_out, rows_out), pl.ds(src, width)],
+            wg_ref.at[:, pl.ds(dst, width)], local_sem.at[5 + n]))
+        own_w[-1].start()
+        aside(fin.at[pl.ds((1 - c) * rows_out, rows_out), pl.ds(src, width)],
+              wg_ref.at[:, pl.ds(dst, width)])
+    loads[3].wait()
+    own_kv.wait()
+    for copy in own_w:
+        copy.wait()
+    for n, copy in enumerate(sides):
+        copy.wait_send()
+        if n >= 4:
+            copy.wait_recv()
+    kv.finish()
+    w.finish()
+    t.finish()
+
+
+def reduce(dkv, dq, xt, scale):
+    tok, dim = dkv.shape[-2:]
+    half = dq.shape[2]
+    features = xt.shape[0]
+    plan = layout(tok, dim, half, features)
+    row_chunk, kv_parts, kv_orders, wide, wide_orders, thin, thin_orders = plan
+    anywhere = pl.BlockSpec(memory_space=pl.ANY)
+    dma = pltpu.SemaphoreType.DMA
+    shapes = (landing_shapes(kv_parts, kv_orders, (2,)) + landing_shapes(wide, wide_orders, ())
+              + landing_shapes(thin, thin_orders, ()))
+    return pl.pallas_call(
+        functools.partial(reduce_kernel, plan, scale),
+        out_shape=(
+            jax.ShapeDtypeStruct((tok, 2 * half), BF16),
+            jax.ShapeDtypeStruct((2, tok, dim), BF16),
+            jax.ShapeDtypeStruct((row_chunk // 2, 2 * half + 2 * dim), F32),
+        ),
+        in_specs=[anywhere] * 3,
+        out_specs=(anywhere,) * 3,
+        scratch_shapes=[
+            pltpu.VMEM(dkv.shape[1:], BF16),
+            pltpu.VMEM(dkv.shape[1:], BF16),
+            pltpu.VMEM((2, tok, dim), BF16),
+            pltpu.VMEM((2,) * 6 + (row_chunk, half), BF16),
+            pltpu.VMEM((2,) * 6 + (row_chunk, dim), BF16),
+            pltpu.VMEM(xt.shape, BF16),
+            pltpu.VMEM(dq.shape, BF16),
+            pltpu.VMEM((row_chunk, half + dim), F32),
+            dma((16,)), dma((16,)), dma((36,)), dma((36,)), dma((24,)), dma((24,)),
+            dma((8,)), dma((8,)), dma((8,)),
+        ] + [pltpu.VMEM(shape, BF16) for shape in shapes],
+        compiler_params=pltpu.CompilerParams(
+            collective_id=2, has_side_effects=True, vmem_limit_bytes=56 * 2**20
+        ),
+        name="reduce",
+    )(dkv, dq, xt)
+
+
+GRAY = (0, 1, 3, 2)
+
+
 def local(
     queries, key_rows, value_rows, forward_out, out_grad, layer_input, doc_lengths, held_span
 ):
     tok = queries.shape[1]
     dim = key_rows.shape[2]
-    heads = queries.shape[2] // dim
-    scale = 1.0 / math.sqrt(dim)
-    ctx = lax.axis_size("ctx")
     me = lax.axis_index("ctx").astype(jnp.int32)
+    z, x = me // 8, lax.rem(me // 2, 4)
+    chip = (z // 2) * 8 + lax.rem(z + z // 2, 2) * 4 + (x // 2) * 2 + lax.rem(x + x // 2, 2)
+    own = jnp.stack([2 * chip, 2 * chip + 1]).astype(jnp.int32)
     ends = jnp.cumsum(doc_lengths[0]).astype(jnp.int32)
-    held = held_span[0]
-    stacked = jnp.stack([key_rows[0], value_rows[0]])
-    both = lax.all_gather(stacked, "ctx", axis=0)
-    k, v = both[:, 0], both[:, 1]
-    delta = jnp.sum(
-        (out_grad[0].astype(F32) * forward_out[0].astype(F32)).reshape(tok, heads, dim), axis=2
-    ).T[None]
-    dq, dk, dv = attention(ends, held, me[None], queries, out_grad, delta, k, v, F32)
-    grads = jnp.concatenate([dk, dv], axis=2).reshape(ctx * tok, 2 * dim)
-    own = lax.psum_scatter(grads, "ctx", scatter_dimension=0, tiled=True)
-    key_local = (scale * own[:, :dim]).astype(BF16)
-    value_local = own[:, dim:].astype(BF16)
-    joined = jnp.concatenate([dq[0], key_local, value_local], axis=1)
-    weight = lax.psum_scatter(
-        lax.dot_general(layer_input[0], joined, (((0,), (0,)), ((), ())), preferred_element_type=F32),
-        ("dp", "ctx"), scatter_dimension=0, tiled=True,
+    held = held_span[0].reshape(4, 4, 2)
+    turned = jnp.stack([held[t] for t in GRAY])
+    held = jnp.stack([turned[:, t] for t in GRAY], axis=1).reshape(-1)
+    k, v, q, do, delta, xt = gather(
+        key_rows[0], value_rows[0], queries[0], out_grad[0], forward_out[0], layer_input[0]
     )
-    return dq, key_local[None], value_local[None], weight
+    dq, dkv = attention(
+        ends, held, own, q, do, delta, k.reshape(-1, tok, dim), v.reshape(-1, tok, dim)
+    )
+    dkv = dkv.reshape(2, 2, 2, 2, 2, 2, tok, dim)
+    qg, kvg, wg = reduce(dkv, dq, xt, 1.0 / math.sqrt(dim))
+    return qg[None], kvg[0][None], kvg[1][None], wg
 
 
 def solution(mesh):
-    from jax.sharding import PartitionSpec as P
     row = P("dp", "ctx", None)
     flat = P("dp", None)
     return jax.shard_map(

time: 933 us -> 156 us (0.17)
  waiting for transfers between devices: 840 us -> 0 us
  Pallas kernels: 20 us -> 133 us
  between operations: 13.8 us -> 0.78 us
  other arithmetic: 13 us -> 1.9 us
  local copies, waits for them, and re-layouts: 30.6 us -> 20.1 us
    unnamed x4 -> x0, waiting for transfers between devices: 665 us -> none
    reduce_scatter x1 -> x0, waiting for transfers between devices: 126 us -> none  [local(): own = lax.psum_scatter(grads, 'ctx', scatter_dimension=0, tiled=True)]
    pallas_call x0 -> x2, Pallas kernels: none -> 110 us  [the longest x1 81.6 us: reduce(): pl.pallas_call(functools.partial(reduce_kernel, plan, scale), out_shape=(...]
    all_gather x1 -> x0, waiting for transfers between devices: 48.6 us -> none  [local(): both = lax.all_gather(stacked, 'ctx', axis=0)]
    unnamed x12 -> x29, local copies, waits for them, and re-layouts: 23.7 us -> 16.7 us
  transfers between devices with their start and end apart: 3 -> 0, of which waited for: 3 -> 0; matrix products, arithmetic and copies ran while one was open for 0% -> 0% of each run, Pallas kernels for 0% -> 0%
where the time goes in v2:
time: 156 us
  Pallas kernels  133 us (85%)
  local copies, waits for them, and re-layouts  20.1 us (13%)
  other arithmetic  1.9 us (1%)
    pallas_call x1, Pallas kernels, reduce(): pl.pallas_call(functools.partial(reduce_kernel, plan, scale), out_shape=(...  81.6 us
    pallas_call x1, Pallas kernels, gather(): pl.pallas_call(gather_kernel, out_shape=(full, full, jax.ShapeDtypeStruct...  28.5 us
    pallas_call x1, Pallas kernels, attention(): pl.pallas_call(functools.partial(attention_kernel, sets, heads, tok, dim,...  22.7 us
    unnamed x29, local copies, waits for them, and re-layouts  16.7 us

profile of v2, /device:TPU:1, one launch (start us, length us, event | category | flops | bytes accessed | tf_op | source)
XLA Modules:
  0.0 155.7 jit_solution(2944515610742237193)
XLA Ops:
  0.7 0.6 pad_add_fusion.1.own_ref
  1.3 1.3 reduce-window.9
  2.6 0.9 slice_reduce_fusion
  3.5 0.1 slice.48
  3.6 0.1 slice.44
  3.9 0.6 reshape.53.held_ref
  4.5 1.6 %copy-done.1 = bf16[1,256,4096]{2,1,0:T(8,128)(2,1)S(1)} copy-done((bf16[1,256,4096]{2,1,0:T(8,128)(2,1)S(1)}, bf16[1,256,4096]{2,1,0:T(8,128)(2,1)}, u32[]{:S(2)}) %copy-start.1) | copy-done | bytes 2097176
  6.1 1.0 copy-done.6
  7.1 1.0 copy-done.7
  8.2 1.0 copy-done.8
  9.2 0.8 copy-done.9
  10.1 0.8 copy-done.10
  10.9 28.5 %gather.1 = (bf16[2,2,2,2,2,256,128]{6,5,4,3,2,1,0:T(8,128)(2,1)S(1)}, bf16[2,2,2,2,2,256,128]{6,5,4,3,2,1,0:T(8,128)(2,1)S(1)}, bf16[2,256,512]{2,1,0:T(8,128)(...) custom-call(bf16[256,128]{1,0:T(8,128)(2,1)S(1)} %bitcast.20, ...), custom_call_target="tpu_custom_call" | custom-call | tf_op jit(solution)/shard_map/gather/pallas_call | solution.py:340
  39.5 1.9 %copy-done = bf16[4096,512]{1,0:T(8,128)(2,1)} copy-done((bf16[4096,512]{1,0:T(8,128)(2,1)}, bf16[4096,512]{1,0:T(8,128)(2,1)S(1)}, u32[]{:S(2)}) %copy-start) | copy-done | bytes 4194328
  41.4 1.4 copy-done.2
  42.7 1.3 copy-done.3
  44.1 0.8 copy-done.4
  44.9 0.8 copy-done.5
  45.7 0.6 copy-done.11
  46.3 22.7 %attention.1 = (bf16[2,256,512]{2,1,0:T(8,128)(2,1)}, bf16[2,32,256,128]{3,2,1,0:T(8,128)(2,1)}) custom-call(s32[4]{0:T(128)} %bitcast.24, s32[32]{0:T(128)} %reshape.53.held_ref, s32[2]{0:T(128)} %pad_add_fusion.1.own_ref, bf16[2,256,512]{2,1,0:T(8,128)(2,1)} %copy-done.4, bf16[2,256,512]{2,1,0:T(8,128)(2,1)} %copy-done.5, f32[2,8,256]{2,1,0:T(8,128)} %copy-done.11, ...), custom_call_target="tpu_custom_call" | custom-call | tf_op jit(solution)/shard_map/attention/pallas_call | solution.py:127
  69.0 81.6 %reduce.17 = (bf16[256,1024]{1,0:T(8,128)(2,1)}, bf16[2,256,128]{2,1,0:T(8,128)(2,1)}, f32[32,1280]{1,0:T(8,128)}) custom-call(bf16[2,2,2,2,2,2,256,128]{7,6,5,4,3,2,1,0:T(8,128)(2,1)} %bitcast.22, bf16[2,256,512]{2,1,0:T(8,128)(2,1)} %get-tuple-element.21.dq_ref, bf16[4096,512]{1,0:T(8,128)(2,1)} %copy-done), custom_call_target="tpu_custom_call" | custom-call | tf_op jit(solution)/shard_map/reduce/pallas_call | solution.py:572
  150.7 1.5 fusion
  152.2 1.9 %copy.17 = bf16[1,256,1024]{2,1,0:T(8,128)(2,1)} copy(bf16[1,256,1024]{2,1,0:T(8,128)(2,1)} %bitcast.23) | data formatting | bytes 1048576
  154.1 1.6 %copy.18 = f32[32,1280]{1,0:T(8,128)} copy(f32[32,1280]{1,0:T(8,128)} %get-tuple-element.41) | data formatting | bytes 327680
  (21 shorter events, 0.2 us)
Async XLA Ops:
  4.5 1.6 %copy-start.1 = (bf16[1,256,4096]{2,1,0:T(8,128)(2,1)S(1)}, bf16[1,256,4096]{2,1,0:T(8,128)(2,1)}, u32[]{:S(2)}) copy-start(bf16[1,256,4096]{2,1,0:T(8,128)(2,1)} %param.13) | copy-start | bytes 6291460
  6.1 1.0 copy-start.6
  7.1 1.0 copy-start.7
  8.2 1.0 copy-start.8
  9.2 0.8 copy-start.9
  10.1 0.8 copy-start.10
  39.4 1.9 %copy-start = (bf16[4096,512]{1,0:T(8,128)(2,1)}, bf16[4096,512]{1,0:T(8,128)(2,1)S(1)}, u32[]{:S(2)}) copy-start(bf16[4096,512]{1,0:T(8,128)(2,1)S(1)} %get-tuple-element.22.xt_ref) | copy-start | bytes 12582916
  41.4 1.4 copy-start.2
  42.7 1.3 copy-start.3
  44.1 0.8 copy-start.4
  44.8 0.8 copy-start.5
  45.7 0.6 copy-start.11

commit v3 on v2

--- a/solution.py
+++ b/solution.py
@@ -15,18 +15,49 @@
     return jnp.dot(a, b, preferred_element_type=F32)
 
 
+def split_axis(t):
+    return t // 2, lax.rem(t + t // 2, 2)
+
+
+def join_bits(bits):
+    return ((bits[0] * 2 + bits[1]) * 2 + bits[2]) * 2 + bits[3]
+
+
 def attention_kernel(sets, heads, tok, dim, blocks,
-                     ends_ref, held_ref, own_ref,
-                     q_ref, do_ref, delta_ref, k_ref, v_ref,
-                     dq_ref, dkv_ref,
-                     qt, dot_, kt, dqt, dka, dva, stat_m, stat_l, bias, seen):
+                     lengths_ref, span_ref,
+                     q_in, do_in, delta_in, k_in, v_in,
+                     dq_out, dkv_out,
+                     qt, dot_, kt, dqt, dka, dva, stat_m, stat_l, bias, seen,
+                     ends_ref, held_ref, q_ref, do_ref, delta_ref, k_ref, v_ref, loads,
+                     dq_ref, dkv_ref, q_stores, kv_stores):
     logit_scale = 1.0 / math.sqrt(dim)
     log2_scale = logit_scale * math.log2(math.e)
 
+    pairs = ((q_in, q_ref), (do_in, do_ref), (delta_in, delta_ref), (k_in, k_ref), (v_in, v_ref))
+    copies = [pltpu.make_async_copy(src, dst, loads.at[n]) for n, (src, dst) in enumerate(pairs)]
+    for copy in copies:
+        copy.start()
+    me = lax.axis_index("ctx")
+    own_chip = join_bits(split_axis(me // 8) + split_axis(lax.rem(me // 2, 4)))
+    doc_count = lengths_ref.shape[1]
+    end = jnp.int32(0)
+    for d in range(doc_count):
+        end = end + lengths_ref[0, d]
+        ends_ref[d] = end
+
+    def place(i, carry):
+        chip = join_bits(split_axis(i // 8) + split_axis(lax.rem(i // 2, 4)))
+        held_ref[2 * chip + lax.rem(i, 2)] = span_ref[0, i]
+        return carry
+
+    lax.fori_loop(0, blocks, place, 0)
     dka[...] = jnp.zeros_like(dka)
     dva[...] = jnp.zeros_like(dva)
+    for copy in copies:
+        copy.wait()
+
     for rs in range(sets):
-        own = own_ref[rs]
+        own = 2 * own_chip + rs
         span = held_ref[own]
         first = span * tok
 
@@ -34,7 +65,6 @@
             end = ends_ref[d]
             return jnp.where(end <= first, jnp.maximum(lo, end), lo)
 
-        doc_count = ends_ref.shape[0]
         lo_first = lax.fori_loop(0, doc_count, count, jnp.int32(0))
         seen[0] = own
 
@@ -109,29 +139,41 @@
         for h in range(heads):
             rows = pl.ds(h * dim, dim)
             dq_ref[rs, :, rows] = (logit_scale * dqt[rows, :]).T.astype(BF16)
+        pltpu.make_async_copy(dq_ref.at[rs], dq_out.at[rs], q_stores.at[rs]).start()
 
     def write(b, carry):
-        dkv_ref[0, b] = dka[b].astype(BF16)
-        dkv_ref[1, b] = dva[b].astype(BF16)
+        for kind, acc in enumerate((dka, dva)):
+            dkv_ref[kind, b] = acc[b].astype(BF16)
+            store(kind, b).start()
         return carry
 
+    def store(kind, b):
+        return pltpu.make_async_copy(dkv_ref.at[kind, b], dkv_out.at[kind, b], kv_stores.at[kind, b])
+
+    def stored(b, carry):
+        store(0, b).wait()
+        store(1, b).wait()
+        return carry
+
     lax.fori_loop(0, blocks, write, 0)
-
-
-def attention(ends, held, own, q, do, delta, k, v):
+    lax.fori_loop(0, blocks, stored, 0)
+    for rs in range(sets):
+        pltpu.make_async_copy(dq_ref.at[rs], dq_out.at[rs], q_stores.at[rs]).wait()
+
+
+def attention(lengths, spans, q, do, delta, k, v):
     sets, tok, width = q.shape
     blocks, _, dim = k.shape
     heads = width // dim
     smem = pl.BlockSpec(memory_space=pltpu.SMEM)
-    vmem = pl.BlockSpec(memory_space=pltpu.VMEM)
     return pl.pallas_call(
         functools.partial(attention_kernel, sets, heads, tok, dim, blocks),
         out_shape=(
             jax.ShapeDtypeStruct(q.shape, BF16),
             jax.ShapeDtypeStruct((2,) + k.shape, BF16),
         ),
-        in_specs=[smem, smem, smem, vmem, vmem, vmem, vmem, vmem],
-        out_specs=(vmem, vmem),
+        in_specs=[smem, smem] + [pl.BlockSpec(memory_space=pltpu.HBM)] * 5,
+        out_specs=(pl.BlockSpec(memory_space=pltpu.HBM),) * 2,
         scratch_shapes=[
             pltpu.VMEM((width, tok), BF16),
             pltpu.VMEM((width, tok), BF16),
@@ -143,14 +185,22 @@
             pltpu.VMEM((heads, tok), F32),
             pltpu.VMEM((tok, tok), F32),
             pltpu.SMEM((blocks + 1,), jnp.int32),
+            pltpu.SMEM((8,), jnp.int32),
+            pltpu.SMEM((blocks,), jnp.int32),
+            pltpu.VMEM(q.shape, BF16),
+            pltpu.VMEM(do.shape, BF16),
+            pltpu.VMEM(delta.shape, F32),
+            pltpu.VMEM(k.shape, BF16),
+            pltpu.VMEM(v.shape, BF16),
+            pltpu.SemaphoreType.DMA((5,)),
+            pltpu.VMEM(q.shape, BF16),
+            pltpu.VMEM((2,) + k.shape, BF16),
+            pltpu.SemaphoreType.DMA((sets,)),
+            pltpu.SemaphoreType.DMA((2, blocks)),
         ],
-        compiler_params=pltpu.CompilerParams(vmem_limit_bytes=56 * 2**20),
+        compiler_params=pltpu.CompilerParams(vmem_limit_bytes=59 * 2**20),
         name="attention",
-    )(ends, held, own, q, do, delta, k, v)
-
-
-def split_axis(t):
-    return t // 2, lax.rem(t + t // 2, 2)
+    )(lengths, spans, q, do, delta, k, v)
 
 
 class Place:
@@ -334,7 +384,7 @@
 def gather(k, v, q, do, o, x):
     tok, dim = k.shape
     half = q.shape[1] // 2
-    anywhere = pl.BlockSpec(memory_space=pl.ANY)
+    anywhere = pl.BlockSpec(memory_space=pltpu.HBM)
     dma = pltpu.SemaphoreType.DMA
     full = jax.ShapeDtypeStruct((2, 2, 2, 2, 2, tok, dim), BF16)
     return pl.pallas_call(
@@ -357,7 +407,7 @@
             dma((32,)), dma((32,)), dma((32,)), dma((32,)), dma((6,)), dma((6,)), dma((9,)),
         ],
         compiler_params=pltpu.CompilerParams(
-            collective_id=1, has_side_effects=True, vmem_limit_bytes=40 * 2**20
+            collective_id=1, has_side_effects=True, vmem_limit_bytes=59 * 2**20
         ),
         name="gather",
     )(k, v, q, do, o, x)
@@ -449,14 +499,14 @@
     w = Halving(here_w, w_acc, wide, wide_orders, landing[n_kv:n_kv + n_w], w_send, w_recv)
     t = Halving(here_w, t_acc, thin, thin_orders, landing[n_kv + n_w:], t_send, t_recv)
 
-    loads = [
-        pltpu.make_async_copy(dq_ref, dq, local_sem.at[0]),
-        pltpu.make_async_copy(xt_ref, xt, local_sem.at[1]),
-        pltpu.make_async_copy(dkv_ref.at[c], kv_acc, local_sem.at[2]),
-        pltpu.make_async_copy(dq_ref.at[c], qg_ref.at[:, pl.ds(c * half, half)], local_sem.at[3]),
-    ]
-    for copy in loads:
-        copy.start()
+    own_q = pltpu.make_async_copy(dq_ref.at[c], qg_ref.at[:, pl.ds(c * half, half)], local_sem.at[3])
+    own_q.start()
+    load_x = pltpu.make_async_copy(xt_ref, xt, local_sem.at[1])
+    load_x.start()
+    load_q = pltpu.make_async_copy(dq_ref, dq, local_sem.at[0])
+    load_q.start()
+    load_kv = pltpu.make_async_copy(dkv_ref.at[c], kv_acc, local_sem.at[2])
+    load_kv.start()
     here_w.greet()
     sides = []
 
@@ -471,7 +521,7 @@
         aside(dkv_ref.at[(1 - c,) + rest + (pl.ds(r0, nr),)], kv_in.at[rest + (pl.ds(r0, nr),)])
     aside(dq_ref.at[1 - c], qg_ref.at[:, pl.ds(c * half, half)])
 
-    loads[2].wait()
+    load_kv.wait()
     for p in range(4):
         r0, nr, _, _ = kv_parts[p]
         sides[p].wait_recv()
@@ -483,9 +533,6 @@
 
         lax.fori_loop(0, 16, join, 0)
         kv.send(p, 0)
-
-    loads[0].wait()
-    loads[1].wait()
 
     def products(i, right, acc):
         block = dot(xt[pl.ds(i * 8 * row_chunk, 8 * row_chunk), :], right).astype(BF16)
@@ -496,6 +543,8 @@
             at = split_axis(y) + split_axis(z) + (x // 2, (x + x // 2) % 2)
             acc[at] = block[j * row_chunk:(j + 1) * row_chunk]
 
+    load_x.wait()
+    load_q.wait()
     both = dq[...].reshape(2 * tok, half)
 
     def wide_products(i, carry):
@@ -546,7 +595,7 @@
         own_w[-1].start()
         aside(fin.at[pl.ds((1 - c) * rows_out, rows_out), pl.ds(src, width)],
               wg_ref.at[:, pl.ds(dst, width)])
-    loads[3].wait()
+    own_q.wait()
     own_kv.wait()
     for copy in own_w:
         copy.wait()
@@ -565,7 +614,6 @@
     features = xt.shape[0]
     plan = layout(tok, dim, half, features)
     row_chunk, kv_parts, kv_orders, wide, wide_orders, thin, thin_orders = plan
-    anywhere = pl.BlockSpec(memory_space=pl.ANY)
     dma = pltpu.SemaphoreType.DMA
     shapes = (landing_shapes(kv_parts, kv_orders, (2,)) + landing_shapes(wide, wide_orders, ())
               + landing_shapes(thin, thin_orders, ()))
@@ -576,8 +624,8 @@
             jax.ShapeDtypeStruct((2, tok, dim), BF16),
             jax.ShapeDtypeStruct((row_chunk // 2, 2 * half + 2 * dim), F32),
         ),
-        in_specs=[anywhere] * 3,
-        out_specs=(anywhere,) * 3,
+        in_specs=[pl.BlockSpec(memory_space=pltpu.HBM)] * 3,
+        out_specs=(pl.BlockSpec(memory_space=pltpu.HBM),) * 3,
         scratch_shapes=[
             pltpu.VMEM(dkv.shape[1:], BF16),
             pltpu.VMEM(dkv.shape[1:], BF16),
@@ -591,13 +639,33 @@
             dma((8,)), dma((8,)), dma((8,)),
         ] + [pltpu.VMEM(shape, BF16) for shape in shapes],
         compiler_params=pltpu.CompilerParams(
-            collective_id=2, has_side_effects=True, vmem_limit_bytes=56 * 2**20
+            collective_id=2, has_side_effects=True, vmem_limit_bytes=58 * 2**20
         ),
         name="reduce",
     )(dkv, dq, xt)
 
 
-GRAY = (0, 1, 3, 2)
+def finish_kernel(qg_ref, kvg_ref, wg_ref, q_out, k_out, v_out, w_out, sems):
+    pairs = ((qg_ref, q_out.at[0]), (kvg_ref.at[0], k_out.at[0]), (kvg_ref.at[1], v_out.at[0]), (wg_ref, w_out))
+    copies = [pltpu.make_async_copy(src, dst, sems.at[n]) for n, (src, dst) in enumerate(pairs)]
+    for copy in copies:
+        copy.start()
+    for copy in copies:
+        copy.wait()
+
+
+def finish(qg, kvg, wg):
+    hbm = pl.BlockSpec(memory_space=pltpu.HBM)
+    one = jax.ShapeDtypeStruct((1,) + kvg.shape[1:], BF16)
+    return pl.pallas_call(
+        finish_kernel,
+        out_shape=(jax.ShapeDtypeStruct((1,) + qg.shape, BF16), one, one, jax.ShapeDtypeStruct(wg.shape, F32)),
+        in_specs=[hbm] * 3,
+        out_specs=(hbm,) * 4,
+        scratch_shapes=[pltpu.SemaphoreType.DMA((4,))],
+        compiler_params=pltpu.CompilerParams(vmem_limit_bytes=60 * 2**20),
+        name="finish",
+    )(qg, kvg, wg)
 
 
 def local(
@@ -605,23 +673,14 @@
 ):
     tok = queries.shape[1]
     dim = key_rows.shape[2]
-    me = lax.axis_index("ctx").astype(jnp.int32)
-    z, x = me // 8, lax.rem(me // 2, 4)
-    chip = (z // 2) * 8 + lax.rem(z + z // 2, 2) * 4 + (x // 2) * 2 + lax.rem(x + x // 2, 2)
-    own = jnp.stack([2 * chip, 2 * chip + 1]).astype(jnp.int32)
-    ends = jnp.cumsum(doc_lengths[0]).astype(jnp.int32)
-    held = held_span[0].reshape(4, 4, 2)
-    turned = jnp.stack([held[t] for t in GRAY])
-    held = jnp.stack([turned[:, t] for t in GRAY], axis=1).reshape(-1)
     k, v, q, do, delta, xt = gather(
         key_rows[0], value_rows[0], queries[0], out_grad[0], forward_out[0], layer_input[0]
     )
     dq, dkv = attention(
-        ends, held, own, q, do, delta, k.reshape(-1, tok, dim), v.reshape(-1, tok, dim)
+        doc_lengths, held_span, q, do, delta, k.reshape(-1, tok, dim), v.reshape(-1, tok, dim)
     )
     dkv = dkv.reshape(2, 2, 2, 2, 2, 2, tok, dim)
-    qg, kvg, wg = reduce(dkv, dq, xt, 1.0 / math.sqrt(dim))
-    return qg[None], kvg[0][None], kvg[1][None], wg
+    return finish(*reduce(dkv, dq, xt, 1.0 / math.sqrt(dim)))
 
 
 def solution(mesh):

time: 156 us -> 186 us (1.19)
  Pallas kernels: 133 us -> 185 us
  local copies, waits for them, and re-layouts: 20.1 us -> 0 us
  other arithmetic: 1.9 us -> 0 us
    pallas_call x0 -> x1, Pallas kernels: none -> 26 us  [finish(): pl.pallas_call(finish_kernel, out_shape=(jax.ShapeDtypeStruct((1,) + qg.s...]
    unnamed x29 -> x0, local copies, waits for them, and re-layouts: 16.7 us -> none
    pallas_call x1, Pallas kernels: 28.5 us -> 44.5 us  [gather(): pl.pallas_call(gather_kernel, out_shape=(full, full, jax.ShapeDtypeStruct...]
    pallas_call x1, Pallas kernels: 22.7 us -> 33.4 us  [attention(): pl.pallas_call(functools.partial(attention_kernel, sets, heads, tok, dim,...]
    slice x8 -> x0, local copies, waits for them, and re-layouts: 2.76 us -> none  [the longest x1 1.53 us: local(): return (qg[None], kvg[0][None], kvg[1][None], wg)]
    another operation x3 -> x0, other arithmetic: 1.9 us -> none
where the time goes in v3:
time: 186 us; the launch traced here: 185 us
  Pallas kernels  185 us (99%)
    pallas_call x1, Pallas kernels, reduce(): pl.pallas_call(functools.partial(reduce_kernel, plan, scale), out_shape=(...  81 us
    pallas_call x1, Pallas kernels, gather(): pl.pallas_call(gather_kernel, out_shape=(full, full, jax.ShapeDtypeStruct...  44.5 us
    pallas_call x1, Pallas kernels, attention(): pl.pallas_call(functools.partial(attention_kernel, sets, heads, tok, dim,...  33.4 us
    pallas_call x1, Pallas kernels, finish(): pl.pallas_call(finish_kernel, out_shape=(jax.ShapeDtypeStruct((1,) + qg.s...  26 us

profile of v3, /device:TPU:1, one launch (start us, length us, event | category | flops | bytes accessed | tf_op | source)
XLA Modules:
  0.0 185.5 jit_solution(15921062594315241457)
XLA Ops:
  0.6 44.5 %gather.1 = (bf16[2,2,2,2,2,256,128]{6,5,4,3,2,1,0:T(8,128)(2,1)}, bf16[2,2,2,2,2,256,128]{6,5,4,3,2,1,0:T(8,128)(2,1)}, bf16[2,256,512]{2,1,0:T(8,128)(2,1)}, b...) custom-call(bf16[256,128]{1,0:T(8,128)(2,1)} %bitcast.16, bf16[256,128]{1,0:T(8,128)(2,1)} %bitcast.17, ...), custom_call_target="tpu_custom_call" | custom-call | tf_op jit(solution)/shard_map/gather/pallas_call | solution.py:390
  45.1 33.4 %attention.1 = (bf16[2,256,512]{2,1,0:T(8,128)(2,1)}, bf16[2,32,256,128]{3,2,1,0:T(8,128)(2,1)}) custom-call(s32[1,4]{1,0:T(1,128)} %lengths_ref.1, s32[1,32]{1,0:T(1,128)} %span_ref.1, bf16[2,256,512]{2,1,0:T(8,128)(2,1)} %get-tuple-element.15.q_in, bf16[2,256,512]{2,1,0:T(8,128)(2,1)} %get-tuple-element.16.do_in, f32[2,8,256]{2,1,0:T(8,128)} %get-tuple-element.17.delta_in, ...), custom_call_target="tpu_custom_call" | custom-call | tf_op jit(solution)/shard_map/attention/pallas_call | solution.py:169
  78.5 81.0 %reduce.1 = (bf16[256,1024]{1,0:T(8,128)(2,1)}, bf16[2,256,128]{2,1,0:T(8,128)(2,1)}, f32[32,1280]{1,0:T(8,128)}) custom-call(bf16[2,2,2,2,2,2,256,128]{7,6,5,4,3,2,1,0:T(8,128)(2,1)} %bitcast.9, bf16[2,256,512]{2,1,0:T(8,128)(2,1)} %get-tuple-element.21.dq_ref, bf16[4096,512]{1,0:T(8,128)(2,1)} %get-tuple-element.22.xt_ref), custom_call_target="tpu_custom_call" | custom-call | tf_op jit(solution)/shard_map/reduce/pallas_call | solution.py:620
  159.5 26.0 %finish.1 = (bf16[1,256,1024]{2,1,0:T(8,128)(2,1)}, bf16[1,256,128]{2,1,0:T(8,128)(2,1)}, bf16[1,256,128]{2,1,0:T(8,128)(2,1)}, f32[32,1280]{1,0:T(8,128)}) custom-call(bf16[256,1024]{1,0:T(8,128)(2,1)} %get-tuple-element.23.qg_ref, bf16[2,256,128]{2,1,0:T(8,128)(2,1)} %get-tuple-element.24.kvg_ref, f32[32,1280]{1,0:T(8,128)} %get-tuple-element.25.wg_ref), custom_call_target="tpu_custom_call" | custom-call | tf_op jit(solution)/shard_map/finish/pallas_call | solution.py:660

commit v4 on v3

--- a/solution.py
+++ b/solution.py
@@ -254,8 +254,8 @@
 
 
 def gather_kernel(k_ref, v_ref, q_ref, do_ref, o_ref, x_ref,
-                  k_all, v_all, q_two, do_two, delta_two, xt_two,
-                  x_buf, do_buf, o_buf, xt_buf, delta_buf,
+                  k_out, v_out, q_two, do_two, delta_two, xt_two,
+                  k_all, v_all, q_buf, x_buf, do_buf, o_buf, xt_buf, delta_buf,
                   hop_send, hop_recv, pass_send, pass_recv, side_send, side_recv, local_sem):
     tok, dim = k_ref.shape
     half = q_two.shape[2]
@@ -265,18 +265,13 @@
     quarter = tok // dims
     sources, targets = (k_ref, v_ref), (k_all, v_all)
 
+    own_k, own_v = k_all.at[here.bits + (c,)], v_all.at[here.bits + (c,)]
     loads = [
-        pltpu.make_async_copy(do_ref, do_buf, local_sem.at[0]),
-        pltpu.make_async_copy(o_ref, o_buf, local_sem.at[1]),
-        pltpu.make_async_copy(x_ref, x_buf, local_sem.at[2]),
+        pltpu.make_async_copy(src, dst, local_sem.at[n])
+        for n, (src, dst) in enumerate((
+            (k_ref, own_k), (v_ref, own_v), (q_ref, q_buf), (do_ref, do_buf), (o_ref, o_buf), (x_ref, x_buf)))
     ]
-    keeps = [
-        pltpu.make_async_copy(k_ref, k_all.at[here.bits + (c,)], local_sem.at[3]),
-        pltpu.make_async_copy(v_ref, v_all.at[here.bits + (c,)], local_sem.at[4]),
-        pltpu.make_async_copy(q_ref.at[:, pl.ds(c * half, half)], q_two.at[c], local_sem.at[5]),
-        pltpu.make_async_copy(do_ref.at[:, pl.ds(c * half, half)], do_two.at[c], local_sem.at[6]),
-    ]
-    for copy in loads + keeps:
+    for copy in loads:
         copy.start()
     here.greet()
 
@@ -294,20 +289,26 @@
             )
             hops[p, 0, kind].start()
     sides = []
-    to_side = [
-        (k_ref, k_all.at[here.bits + (c,)]),
-        (v_ref, v_all.at[here.bits + (c,)]),
-        (q_ref.at[:, pl.ds((1 - c) * half, half)], q_two.at[c]),
-        (do_ref.at[:, pl.ds((1 - c) * half, half)], do_two.at[c]),
-    ]
-
     def aside(src, dst):
         n = len(sides)
         sides.append(remote(src, dst, side_send.at[n], side_recv.at[n], here.sibling))
         sides[-1].start()
 
-    for src, dst in to_side:
-        aside(src, dst)
+    for copy in loads[:5]:
+        copy.wait()
+    theirs, mine = pl.ds((1 - c) * half, half), pl.ds(c * half, half)
+    aside(own_k, own_k)
+    aside(own_v, own_v)
+    aside(q_buf.at[:, theirs], q_two.at[c])
+    aside(do_buf.at[:, theirs], do_two.at[c])
+    keeps = []
+
+    def keep(src, dst):
+        keeps.append(pltpu.make_async_copy(src, dst, local_sem.at[6 + len(keeps)]))
+        keeps[-1].start()
+
+    keep(q_buf.at[:, mine], q_two.at[c])
+    keep(do_buf.at[:, mine], do_two.at[c])
 
     passes = []
 
@@ -331,11 +332,6 @@
             )
             hops[p, s, kind].start()
 
-    for copy in keeps:
-        copy.wait()
-
-    loads[0].wait()
-    loads[1].wait()
     heads = half // dim
     for h in range(2 * heads):
         cols = pl.ds(h * dim, dim)
@@ -343,14 +339,13 @@
         delta_buf[h // heads, pl.ds(h % heads, 1), :] = jnp.sum(products.T, axis=0, keepdims=True)
     for h in range(heads, delta_buf.shape[1]):
         delta_buf[:, pl.ds(h, 1), :] = jnp.zeros((2, 1, tok), F32)
-    own_delta = pltpu.make_async_copy(delta_buf.at[c], delta_two.at[c], local_sem.at[7])
-    own_delta.start()
+    keep(delta_buf.at[c], delta_two.at[c])
     aside(delta_buf.at[1 - c], delta_two.at[c])
 
     for p in range(dims):
         hand_on(p, 0)
         hop(p, 1)
-    loads[2].wait()
+    loads[5].wait()
 
     def turn(i, carry):
         xt_buf[pl.ds(i * 128, 128), :] = x_buf[:, pl.ds(i * 128, 128)].T
@@ -363,21 +358,25 @@
         hop(p, 2)
     lax.fori_loop(steps // 2, steps, turn, 0)
     mine = xt_two.at[:, pl.ds(c * tok, tok)]
-    own_xt = pltpu.make_async_copy(xt_buf, mine, local_sem.at[8])
-    own_xt.start()
+    keep(xt_buf, mine)
     for p in range(dims):
         hand_on(p, 2)
         hop(p, 3)
     aside(xt_buf, mine)
     for p in range(dims):
         hand_on(p, 3)
-    own_delta.wait()
-    own_xt.wait()
-    for copy in hops.values():
-        copy.wait_send()
+    everywhere = (slice(None),) * dims
+    keep(k_all.at[everywhere + (c,)], k_out.at[everywhere + (c,)])
+    keep(v_all.at[everywhere + (c,)], v_out.at[everywhere + (c,)])
     for copy in passes:
         copy.wait()
     for copy in sides:
+        copy.wait()
+    keep(k_all.at[everywhere + (1 - c,)], k_out.at[everywhere + (1 - c,)])
+    keep(v_all.at[everywhere + (1 - c,)], v_out.at[everywhere + (1 - c,)])
+    for copy in hops.values():
+        copy.wait_send()
+    for copy in keeps:
         copy.wait()
 
 
@@ -399,12 +398,15 @@
         in_specs=[anywhere] * 6,
         out_specs=(anywhere,) * 6,
         scratch_shapes=[
+            pltpu.VMEM(full.shape, BF16),
+            pltpu.VMEM(full.shape, BF16),
+            pltpu.VMEM(q.shape, BF16),
             pltpu.VMEM(x.shape, BF16),
             pltpu.VMEM(q.shape, BF16),
             pltpu.VMEM(q.shape, BF16),
             pltpu.VMEM((x.shape[1], tok), BF16),
             pltpu.VMEM((2, 8, tok), F32),
-            dma((32,)), dma((32,)), dma((32,)), dma((32,)), dma((6,)), dma((6,)), dma((9,)),
+            dma((32,)), dma((32,)), dma((32,)), dma((32,)), dma((6,)), dma((6,)), dma((14,)),
         ],
         compiler_params=pltpu.CompilerParams(
             collective_id=1, has_side_effects=True, vmem_limit_bytes=59 * 2**20
@@ -499,8 +501,6 @@
     w = Halving(here_w, w_acc, wide, wide_orders, landing[n_kv:n_kv + n_w], w_send, w_recv)
     t = Halving(here_w, t_acc, thin, thin_orders, landing[n_kv + n_w:], t_send, t_recv)
 
-    own_q = pltpu.make_async_copy(dq_ref.at[c], qg_ref.at[:, pl.ds(c * half, half)], local_sem.at[3])
-    own_q.start()
     load_x = pltpu.make_async_copy(xt_ref, xt, local_sem.at[1])
     load_x.start()
     load_q = pltpu.make_async_copy(dq_ref, dq, local_sem.at[0])
@@ -545,6 +545,8 @@
 
     load_x.wait()
     load_q.wait()
+    own_q = pltpu.make_async_copy(dq.at[c], qg_ref.at[:, pl.ds(c * half, half)], local_sem.at[3])
+    own_q.start()
     both = dq[...].reshape(2 * tok, half)
 
     def wide_products(i, carry):
@@ -660,10 +662,10 @@
     return pl.pallas_call(
         finish_kernel,
         out_shape=(jax.ShapeDtypeStruct((1,) + qg.shape, BF16), one, one, jax.ShapeDtypeStruct(wg.shape, F32)),
-        in_specs=[hbm] * 3,
+        in_specs=[pl.BlockSpec(memory_space=pltpu.VMEM)] * 3,
         out_specs=(hbm,) * 4,
         scratch_shapes=[pltpu.SemaphoreType.DMA((4,))],
-        compiler_params=pltpu.CompilerParams(vmem_limit_bytes=60 * 2**20),
+        compiler_params=pltpu.CompilerParams(vmem_limit_bytes=59 * 2**20),
         name="finish",
     )(qg, kvg, wg)
 

time: 186 us -> 144 us (0.77)
  Pallas kernels: 185 us -> 143 us
    pallas_call x1, Pallas kernels: 26 us -> 2.06 us  [finish(): pl.pallas_call(finish_kernel, out_shape=(jax.ShapeDtypeStruct((1,) + qg.s...]
    pallas_call x1, Pallas kernels: 44.5 us -> 29.9 us  [gather(): pl.pallas_call(gather_kernel, out_shape=(full, full, jax.ShapeDtypeStruct...]
    pallas_call x1, Pallas kernels: 33.4 us -> 28.7 us  [attention(): pl.pallas_call(functools.partial(attention_kernel, sets, heads, tok, dim,...]
where the time goes in v4:
time: 144 us; the launch traced here: 143 us
  Pallas kernels  143 us (99%)
    pallas_call x1, Pallas kernels, reduce(): pl.pallas_call(functools.partial(reduce_kernel, plan, scale), out_shape=(...  82.2 us
    pallas_call x1, Pallas kernels, gather(): pl.pallas_call(gather_kernel, out_shape=(full, full, jax.ShapeDtypeStruct...  29.9 us
    pallas_call x1, Pallas kernels, attention(): pl.pallas_call(functools.partial(attention_kernel, sets, heads, tok, dim,...  28.7 us

profile of v4, /device:TPU:1, one launch (start us, length us, event | category | flops | bytes accessed | tf_op | source)
XLA Modules:
  0.0 143.5 jit_solution(12858883674437059532)
XLA Ops:
  0.6 29.9 %gather.1 = (bf16[2,2,2,2,2,256,128]{6,5,4,3,2,1,0:T(8,128)(2,1)}, bf16[2,2,2,2,2,256,128]{6,5,4,3,2,1,0:T(8,128)(2,1)}, bf16[2,256,512]{2,1,0:T(8,128)(2,1)}, b...) custom-call(bf16[256,128]{1,0:T(8,128)(2,1)} %bitcast.16, bf16[256,128]{1,0:T(8,128)(2,1)} %bitcast.17, ...), custom_call_target="tpu_custom_call" | custom-call | tf_op jit(solution)/shard_map/gather/pallas_call | solution.py:389
  30.5 28.7 %attention.1 = (bf16[2,256,512]{2,1,0:T(8,128)(2,1)}, bf16[2,32,256,128]{3,2,1,0:T(8,128)(2,1)}) custom-call(s32[1,4]{1,0:T(1,128)} %lengths_ref.1, s32[1,32]{1,0:T(1,128)} %span_ref.1, bf16[2,256,512]{2,1,0:T(8,128)(2,1)} %get-tuple-element.15.q_in, bf16[2,256,512]{2,1,0:T(8,128)(2,1)} %get-tuple-element.16.do_in, f32[2,8,256]{2,1,0:T(8,128)} %get-tuple-element.17.delta_in, ...), custom_call_target="tpu_custom_call" | custom-call | tf_op jit(solution)/shard_map/attention/pallas_call | solution.py:169
  59.2 82.2 %reduce.1 = (bf16[256,1024]{1,0:T(8,128)(2,1)}, bf16[2,256,128]{2,1,0:T(8,128)(2,1)}, f32[32,1280]{1,0:T(8,128)}) custom-call(bf16[2,2,2,2,2,2,256,128]{7,6,5,4,3,2,1,0:T(8,128)(2,1)} %bitcast.9, bf16[2,256,512]{2,1,0:T(8,128)(2,1)} %get-tuple-element.21.dq_ref, bf16[4096,512]{1,0:T(8,128)(2,1)} %get-tuple-element.22.xt_ref), custom_call_target="tpu_custom_call" | custom-call | tf_op jit(solution)/shard_map/reduce/pallas_call | solution.py:622
  141.4 2.1 %finish.1 = (bf16[1,256,1024]{2,1,0:T(8,128)(2,1)}, bf16[1,256,128]{2,1,0:T(8,128)(2,1)}, bf16[1,256,128]{2,1,0:T(8,128)(2,1)}, f32[32,1280]{1,0:T(8,128)}) custom-call(bf16[256,1024]{1,0:T(8,128)(2,1)} %get-tuple-element.23.qg_ref, bf16[2,256,128]{2,1,0:T(8,128)(2,1)} %get-tuple-element.24.kvg_ref, f32[32,1280]{1,0:T(8,128)} %get-tuple-element.25.wg_ref), custom_call_target="tpu_custom_call" | custom-call | tf_op jit(solution)/shard_map/finish/pallas_call | solution.py:662

commit v5 on v4

--- a/solution.py
+++ b/solution.py
@@ -9,6 +9,7 @@
 BF16 = jnp.bfloat16
 MESH = pl.DeviceIdType.MESH
 NEG = -1e30
+LONGEST = 4096
 
 
 def dot(a, b):
@@ -29,7 +30,8 @@
                      dq_out, dkv_out,
                      qt, dot_, kt, dqt, dka, dva, stat_m, stat_l, bias, seen,
                      ends_ref, held_ref, q_ref, do_ref, delta_ref, k_ref, v_ref, loads,
-                     dq_ref, dkv_ref, q_stores, kv_stores):
+                     dq_ref, dkv_ref, q_stores, kv_stores,
+                     q_flat, do_flat, kept, kept_m, p_all, ds_all, marked):
     logit_scale = 1.0 / math.sqrt(dim)
     log2_scale = logit_scale * math.log2(math.e)
 
@@ -53,6 +55,14 @@
     lax.fori_loop(0, blocks, place, 0)
     dka[...] = jnp.zeros_like(dka)
     dva[...] = jnp.zeros_like(dva)
+    def store(kind, b):
+        return pltpu.make_async_copy(dkv_ref.at[kind, b], dkv_out.at[kind, b], kv_stores.at[kind, b])
+
+    def write(b):
+        for kind, acc in enumerate((dka, dva)):
+            dkv_ref[kind, b] = acc[b].astype(BF16)
+            store(kind, b).start()
+
     for copy in copies:
         copy.wait()
 
@@ -79,10 +89,33 @@
             return n + take.astype(jnp.int32)
 
         total = lax.fori_loop(0, blocks, collect, jnp.int32(1))
+        last = rs == sets - 1
+        if last:
+            def unmark(b, carry):
+                marked[b] = 0
+                return carry
+
+            def mark(i, carry):
+                marked[seen[i]] = 1
+                return carry
+
+            def write_other(b, carry):
+                @pl.when(marked[b] == 0)
+                def _():
+                    write(b)
+
+                return carry
+
+            lax.fori_loop(0, blocks, unmark, 0)
+            lax.fori_loop(0, total, mark, 0)
+            lax.fori_loop(0, blocks, write_other, 0)
         for h in range(heads):
             rows = pl.ds(h * dim, dim)
-            qt[rows, :] = q_ref[rs, :, rows].T
-            dot_[rows, :] = do_ref[rs, :, rows].T
+            flat = pl.ds(h * tok, tok)
+            q_flat[flat, :] = q_ref[rs, :, rows]
+            do_flat[flat, :] = do_ref[rs, :, rows]
+            qt[:, flat] = q_flat[flat, :].T
+            dot_[:, flat] = do_flat[flat, :].T
         pos = first + lax.broadcasted_iota(jnp.int32, (1, tok), 1)
         low = jnp.zeros((1, tok), jnp.int32)
         for d in range(doc_count):
@@ -103,12 +136,16 @@
             k = k_ref[b]
             kt[b] = k.T
             for h in range(heads):
-                s = dot(k, qt[pl.ds(h * dim, dim), :]) * log2_scale + bias[...]
-                m_old = stat_m[pl.ds(h, 1), :]
+                row, cols = pl.ds(h, 1), pl.ds(h * tok, tok)
+                s = dot(k, qt[:, cols]) * log2_scale + bias[...]
+                m_old = stat_m[row, :]
                 m_new = jnp.maximum(m_old, jnp.max(s, axis=0, keepdims=True))
-                add = jnp.sum(jnp.exp2(s - m_new), axis=0, keepdims=True)
-                stat_l[pl.ds(h, 1), :] = stat_l[pl.ds(h, 1), :] * jnp.exp2(m_old - m_new) + add
-                stat_m[pl.ds(h, 1), :] = m_new
+                p = jnp.exp2(s - m_new)
+                kept[i, :, cols] = p.astype(BF16)
+                add = jnp.sum(p, axis=0, keepdims=True)
+                stat_l[row, :] = stat_l[row, :] * jnp.exp2(m_old - m_new) + add
+                stat_m[row, :] = m_new
+                kept_m[i, row, :] = m_new
             return carry
 
         lax.fori_loop(0, total, pass_one, 0)
@@ -116,46 +153,32 @@
 
         def pass_two(i, carry):
             b = seen[i]
-            set_bias(b)
-            k = k_ref[b]
             v = v_ref[b]
-            ktb = kt[b]
-            dk = dka[b]
-            dv = dva[b]
             for h in range(heads):
-                rows = pl.ds(h * dim, dim)
-                s = dot(k, qt[rows, :]) * log2_scale + bias[...]
-                p = jnp.exp2(s - stat_m[pl.ds(h, 1), :])
-                dp = dot(v, dot_[rows, :])
-                ds = (p * (dp - delta_ref[rs, pl.ds(h, 1), :])).astype(BF16)
-                dv = dv + dot(p.astype(BF16), do_ref[rs, :, rows])
-                dk = dk + dot(ds, q_ref[rs, :, rows])
-                dqt[rows, :] += dot(ktb, ds)
-            dka[b] = dk
-            dva[b] = dv
+                row, cols = pl.ds(h, 1), pl.ds(h * tok, tok)
+                scaled = jnp.exp2(kept_m[i, row, :] - stat_m[row, :])
+                p = kept[i, :, cols].astype(F32) * scaled
+                dp = dot(v, dot_[:, cols])
+                p_all[:, cols] = p.astype(BF16)
+                ds_all[:, cols] = (p * (dp - delta_ref[rs, row, :])).astype(BF16)
+            dva[b] += dot(p_all[...], do_flat[...])
+            dka[b] += dot(ds_all[...], q_flat[...])
+            dqt[...] += dot(kt[b], ds_all[...])
+            if last:
+                write(b)
             return carry
 
         lax.fori_loop(0, total, pass_two, 0)
         for h in range(heads):
             rows = pl.ds(h * dim, dim)
-            dq_ref[rs, :, rows] = (logit_scale * dqt[rows, :]).T.astype(BF16)
+            dq_ref[rs, :, rows] = (logit_scale * dqt[:, pl.ds(h * tok, tok)]).T.astype(BF16)
         pltpu.make_async_copy(dq_ref.at[rs], dq_out.at[rs], q_stores.at[rs]).start()
-
-    def write(b, carry):
-        for kind, acc in enumerate((dka, dva)):
-            dkv_ref[kind, b] = acc[b].astype(BF16)
-            store(kind, b).start()
-        return carry
-
-    def store(kind, b):
-        return pltpu.make_async_copy(dkv_ref.at[kind, b], dkv_out.at[kind, b], kv_stores.at[kind, b])
 
     def stored(b, carry):
         store(0, b).wait()
         store(1, b).wait()
         return carry
 
-    lax.fori_loop(0, blocks, write, 0)
     lax.fori_loop(0, blocks, stored, 0)
     for rs in range(sets):
         pltpu.make_async_copy(dq_ref.at[rs], dq_out.at[rs], q_stores.at[rs]).wait()
@@ -175,10 +198,10 @@
         in_specs=[smem, smem] + [pl.BlockSpec(memory_space=pltpu.HBM)] * 5,
         out_specs=(pl.BlockSpec(memory_space=pltpu.HBM),) * 2,
         scratch_shapes=[
-            pltpu.VMEM((width, tok), BF16),
-            pltpu.VMEM((width, tok), BF16),
+            pltpu.VMEM((dim, heads * tok), BF16),
+            pltpu.VMEM((dim, heads * tok), BF16),
             pltpu.VMEM((blocks, dim, tok), BF16),
-            pltpu.VMEM((width, tok), F32),
+            pltpu.VMEM((dim, heads * tok), F32),
             pltpu.VMEM((blocks, tok, dim), F32),
             pltpu.VMEM((blocks, tok, dim), F32),
             pltpu.VMEM((heads, tok), F32),
@@ -197,6 +220,13 @@
             pltpu.VMEM((2,) + k.shape, BF16),
             pltpu.SemaphoreType.DMA((sets,)),
             pltpu.SemaphoreType.DMA((2, blocks)),
+            pltpu.VMEM((heads * tok, dim), BF16),
+            pltpu.VMEM((heads * tok, dim), BF16),
+            pltpu.VMEM((LONGEST // tok + 1, tok, heads * tok), BF16),
+            pltpu.VMEM((LONGEST // tok + 1, heads, tok), F32),
+            pltpu.VMEM((tok, heads * tok), BF16),
+            pltpu.VMEM((tok, heads * tok), BF16),
+            pltpu.SMEM((blocks,), jnp.int32),
         ],
         compiler_params=pltpu.CompilerParams(vmem_limit_bytes=59 * 2**20),
         name="attention",
@@ -217,26 +247,32 @@
         def low(t):
             return t + 1 - 2 * lax.rem(t, 2)
 
+        def far(t):
+            return lax.rem(t + 2, 4)
+
+        self.opposite = ()
         self.bits = split_axis(z) + split_axis(x)
         self.partners = (at(y, 3 - z, x), at(y, low(z), x), at(y, z, 3 - x), at(y, z, low(x)))
         if with_dp:
             self.bits = split_axis(y) + self.bits
             self.partners = (at(3 - y, z, x), at(low(y), z, x)) + self.partners
+            self.opposite = tuple(
+                at(*t) for t in ((far(y), z, x), (y, far(z), x), (y, z, far(x))))
         self.dims = len(self.bits)
 
     def greet(self):
         barrier = pltpu.get_barrier_semaphore()
-        everyone = (self.sibling,) + self.partners
+        everyone = (self.sibling,) + self.partners + self.opposite
         for other in everyone:
             pl.semaphore_signal(barrier, inc=1, device_id=other, device_id_type=MESH)
         pl.semaphore_wait(barrier, len(everyone))
 
-    def spot(self, free, flipped=None):
+    def spot(self, free, flipped=()):
         found = []
         for d in range(self.dims):
             if d in free:
                 found.append(slice(None))
-            elif d == flipped:
+            elif d in flipped:
                 found.append(1 - self.bits[d])
             else:
                 found.append(self.bits[d])
@@ -317,7 +353,7 @@
         for kind in range(2):
             n = (p * dims + s) * 2 + kind
             hops[p, s, kind].wait_recv()
-            part = targets[kind].at[here.spot(order[:s], order[s]) + (c,) + rows(p)]
+            part = targets[kind].at[here.spot(order[:s], (order[s],)) + (c,) + rows(p)]
             copy = remote(part, part, pass_send.at[n], pass_recv.at[n], here.sibling)
             copy.start()
             passes.append(copy)
@@ -332,6 +368,9 @@
             )
             hops[p, s, kind].start()
 
+    for p in range(dims):
+        hand_on(p, 0)
+        hop(p, 1)
     heads = half // dim
     for h in range(2 * heads):
         cols = pl.ds(h * dim, dim)
@@ -341,10 +380,6 @@
         delta_buf[:, pl.ds(h, 1), :] = jnp.zeros((2, 1, tok), F32)
     keep(delta_buf.at[c], delta_two.at[c])
     aside(delta_buf.at[1 - c], delta_two.at[c])
-
-    for p in range(dims):
-        hand_on(p, 0)
-        hop(p, 1)
     loads[5].wait()
 
     def turn(i, carry):
@@ -352,16 +387,16 @@
         return carry
 
     steps = x_ref.shape[1] // 128
-    lax.fori_loop(0, steps // 2, turn, 0)
     for p in range(dims):
         hand_on(p, 1)
         hop(p, 2)
-    lax.fori_loop(steps // 2, steps, turn, 0)
+    lax.fori_loop(0, steps // 2, turn, 0)
     mine = xt_two.at[:, pl.ds(c * tok, tok)]
-    keep(xt_buf, mine)
     for p in range(dims):
         hand_on(p, 2)
         hop(p, 3)
+    lax.fori_loop(steps // 2, steps, turn, 0)
+    keep(xt_buf, mine)
     aside(xt_buf, mine)
     for p in range(dims):
         hand_on(p, 3)
@@ -427,6 +462,11 @@
     return [(i * (rows // 4), rows // 4, 0, cols) for i in range(4)]
 
 
+def ring_parts(rows, cols):
+    half, quarter = rows // 2, rows // 4
+    return [(0, half, 0, cols), (half, quarter, 0, cols), (half + quarter, quarter, 0, cols)]
+
+
 class Halving:
     def __init__(self, here, acc, parts, orders, landing, send, recv):
         self.here, self.acc, self.parts, self.orders = here, acc, parts, orders
@@ -438,7 +478,7 @@
         order = self.orders[p]
         free = order[s + 1:]
         d = order[s]
-        return self.here.spot(free, d if flip else None) + self.cut(r0, nr, c0, nc)
+        return self.here.spot(free, (d,) if flip else ()) + self.cut(r0, nr, c0, nc)
 
     def cut(self, r0, nr, c0, nc):
         return (slice(None),) * (len(self.acc.shape) - self.here.dims - 2) + (
@@ -467,6 +507,51 @@
             copy.wait_send()
 
 
+class Rings:
+    def __init__(self, here, acc, parts, orders, landing, send, recv):
+        self.here, self.acc, self.parts, self.orders = here, acc, parts, orders
+        self.landing, self.send_sem, self.recv_sem = landing, send, recv
+        self.copies = {}
+
+    def index(self, p, s, flipped):
+        r0, nr, c0, nc = self.parts[p]
+        free = [d for a in self.orders[p][s + 1:] for d in (2 * a, 2 * a + 1)]
+        return self.here.spot(free, flipped) + (pl.ds(r0, nr), pl.ds(c0, nc))
+
+    def send(self, p, s):
+        a = self.orders[p][s]
+        high, low = 2 * a, 2 * a + 1
+        ways = (((low,), self.here.partners[low]), ((high,), self.here.partners[high]),
+                ((high, low), self.here.opposite[a]))
+        for m in (2, 0, 1):
+            flipped, partner = ways[m]
+            n = (p * 3 + s) * 3 + m
+            copy = remote(
+                self.acc.at[self.index(p, s, flipped)], self.landing[n],
+                self.send_sem.at[n], self.recv_sem.at[n], partner,
+            )
+            copy.start()
+            self.copies[p, s, m] = copy
+
+    def total(self, p, s):
+        found = self.acc[self.index(p, s, ())].astype(F32)
+        for m in range(3):
+            self.copies[p, s, m].wait_recv()
+            found = found + self.landing[(p * 3 + s) * 3 + m][...].astype(F32)
+        return found
+
+    def add(self, p, s):
+        self.acc[self.index(p, s, ())] = self.total(p, s).astype(self.acc.dtype)
+
+    def finish(self):
+        for copy in self.copies.values():
+            copy.wait_send()
+
+
+def ring_shapes(parts):
+    return [(2,) * (2 * (2 - s)) + (nr, nc) for (_, nr, _, nc) in parts for s in range(3) for _ in range(3)]
+
+
 def landing_shapes(parts, orders, extra):
     shapes = []
     for (_, nr, _, nc), order in zip(parts, orders):
@@ -481,8 +566,8 @@
     kv_orders = [turns(4, p) for p in range(4)]
     wide = wide_parts(row_chunk, half)
     wide_orders = [turns(6, p) for p in range(6)]
-    thin = thin_parts(row_chunk, dim)
-    thin_orders = [turns(6, p) for p in (0, 2, 3, 5)]
+    thin = ring_parts(row_chunk, dim)
+    thin_orders = [turns(3, p) for p in range(3)]
     return row_chunk, kv_parts, kv_orders, wide, wide_orders, thin, thin_orders
 
 
@@ -499,7 +584,7 @@
     n_kv, n_w = 16, 36
     kv = Halving(here, kv_acc, kv_parts, kv_orders, landing[:n_kv], kv_send, kv_recv)
     w = Halving(here_w, w_acc, wide, wide_orders, landing[n_kv:n_kv + n_w], w_send, w_recv)
-    t = Halving(here_w, t_acc, thin, thin_orders, landing[n_kv + n_w:], t_send, t_recv)
+    t = Rings(here_w, t_acc, thin, thin_orders, landing[n_kv + n_w:], t_send, t_recv)
 
     load_x = pltpu.make_async_copy(xt_ref, xt, local_sem.at[1])
     load_x.start()
@@ -556,10 +641,17 @@
     lax.fori_loop(0, 8, wide_products, 0)
     for p in range(6):
         w.send(p, 0)
+    def wide_step(s):
+        for p in range(6):
+            w.add(p, s - 1)
+            w.send(p, s)
+
     for s in range(1, 4):
         for p in range(4):
             kv.add(p, s - 1)
             kv.send(p, s)
+        if s > 1:
+            wide_step(s - 1)
     kv_scale = jnp.where(c == 0, scale, 1.0).astype(F32)
     for p in range(4):
         r0, nr, _, _ = kv_parts[p]
@@ -574,19 +666,18 @@
         return carry
 
     lax.fori_loop(0, 8, thin_products, 0)
-    for p in range(4):
+    for p in range(3):
         t.send(p, 0)
-    for s in range(1, 6):
-        for p in range(6):
-            w.add(p, s - 1)
-            w.send(p, s)
-        for p in range(4):
+    wide_step(3)
+    for s in range(1, 3):
+        for p in range(3):
             t.add(p, s - 1)
             t.send(p, s)
+        wide_step(s + 3)
     for p, (r0, nr, c0, nc) in enumerate(wide):
         fin[pl.ds(r0, nr), pl.ds(c0, nc)] = w.total(p, 5)
     for p, (r0, nr, c0, nc) in enumerate(thin):
-        fin[pl.ds(r0, nr), pl.ds(half, nc)] = t.total(p, 5)
+        fin[pl.ds(r0, nr), pl.ds(half, nc)] = t.total(p, 2)
     rows_out = row_chunk // 2
     pieces = [(0, c * half, half), (half, 2 * half + c * dim, dim)]
     own_w = []
@@ -618,7 +709,7 @@
     row_chunk, kv_parts, kv_orders, wide, wide_orders, thin, thin_orders = plan
     dma = pltpu.SemaphoreType.DMA
     shapes = (landing_shapes(kv_parts, kv_orders, (2,)) + landing_shapes(wide, wide_orders, ())
-              + landing_shapes(thin, thin_orders, ()))
+              + ring_shapes(thin))
     return pl.pallas_call(
         functools.partial(reduce_kernel, plan, scale),
         out_shape=(
@@ -637,7 +728,7 @@
             pltpu.VMEM(xt.shape, BF16),
             pltpu.VMEM(dq.shape, BF16),
             pltpu.VMEM((row_chunk, half + dim), F32),
-            dma((16,)), dma((16,)), dma((36,)), dma((36,)), dma((24,)), dma((24,)),
+            dma((16,)), dma((16,)), dma((36,)), dma((36,)), dma((27,)), dma((27,)),
             dma((8,)), dma((8,)), dma((8,)),
         ] + [pltpu.VMEM(shape, BF16) for shape in shapes],
         compiler_params=pltpu.CompilerParams(

time: 144 us -> 126 us (0.88)
  Pallas kernels: 143 us -> 125 us
    pallas_call x1, Pallas kernels: 82.2 us -> 68.4 us  [reduce(): pl.pallas_call(functools.partial(reduce_kernel, plan, scale), out_shape=(...]
    pallas_call x1, Pallas kernels: 28.7 us -> 25 us  [attention(): pl.pallas_call(functools.partial(attention_kernel, sets, heads, tok, dim,...]
where the time goes in v5:
time: 126 us
  Pallas kernels  125 us (99%)
    pallas_call x1, Pallas kernels, reduce(): pl.pallas_call(functools.partial(reduce_kernel, plan, scale), out_shape=(...  68.4 us
    pallas_call x1, Pallas kernels, gather(): pl.pallas_call(gather_kernel, out_shape=(full, full, jax.ShapeDtypeStruct...  29.7 us
    pallas_call x1, Pallas kernels, attention(): pl.pallas_call(functools.partial(attention_kernel, sets, heads, tok, dim,...  25 us

profile of v5, /device:TPU:1, one launch (start us, length us, event | category | flops | bytes accessed | tf_op | source)
XLA Modules:
  0.0 125.9 jit_solution(16540896027012472430)
XLA Ops:
  0.6 29.7 %gather.1 = (bf16[2,2,2,2,2,256,128]{6,5,4,3,2,1,0:T(8,128)(2,1)}, bf16[2,2,2,2,2,256,128]{6,5,4,3,2,1,0:T(8,128)(2,1)}, bf16[2,256,512]{2,1,0:T(8,128)(2,1)}, b...) custom-call(bf16[256,128]{1,0:T(8,128)(2,1)} %bitcast.16, bf16[256,128]{1,0:T(8,128)(2,1)} %bitcast.17, ...), custom_call_target="tpu_custom_call" | custom-call | tf_op jit(solution)/shard_map/gather/pallas_call | solution.py:424
  30.4 25.0 %attention.1 = (bf16[2,256,512]{2,1,0:T(8,128)(2,1)}, bf16[2,32,256,128]{3,2,1,0:T(8,128)(2,1)}) custom-call(s32[1,4]{1,0:T(1,128)} %lengths_ref.1, s32[1,32]{1,0:T(1,128)} %span_ref.1, bf16[2,256,512]{2,1,0:T(8,128)(2,1)} %get-tuple-element.15.q_in, bf16[2,256,512]{2,1,0:T(8,128)(2,1)} %get-tuple-element.16.do_in, f32[2,8,256]{2,1,0:T(8,128)} %get-tuple-element.17.delta_in, ...), custom_call_target="tpu_custom_call" | custom-call | tf_op jit(solution)/shard_map/attention/pallas_call | solution.py:192
  55.4 68.4 %reduce.1 = (bf16[256,1024]{1,0:T(8,128)(2,1)}, bf16[2,256,128]{2,1,0:T(8,128)(2,1)}, f32[32,1280]{1,0:T(8,128)}) custom-call(bf16[2,2,2,2,2,2,256,128]{7,6,5,4,3,2,1,0:T(8,128)(2,1)} %bitcast.9, bf16[2,256,512]{2,1,0:T(8,128)(2,1)} %get-tuple-element.21.dq_ref, bf16[4096,512]{1,0:T(8,128)(2,1)} %get-tuple-element.22.xt_ref), custom_call_target="tpu_custom_call" | custom-call | tf_op jit(solution)/shard_map/reduce/pallas_call | solution.py:713
  123.8 2.1 %finish.1 = (bf16[1,256,1024]{2,1,0:T(8,128)(2,1)}, bf16[1,256,128]{2,1,0:T(8,128)(2,1)}, bf16[1,256,128]{2,1,0:T(8,128)(2,1)}, f32[32,1280]{1,0:T(8,128)}) custom-call(bf16[256,1024]{1,0:T(8,128)(2,1)} %get-tuple-element.23.qg_ref, bf16[2,256,128]{2,1,0:T(8,128)(2,1)} %get-tuple-element.24.kvg_ref, f32[32,1280]{1,0:T(8,128)} %get-tuple-element.25.wg_ref), custom_call_target="tpu_custom_call" | custom-call | tf_op jit(solution)/shard_map/finish/pallas_call | solution.py:753

commit v6 on v5

--- a/solution.py
+++ b/solution.py
@@ -250,19 +250,18 @@
         def far(t):
             return lax.rem(t + 2, 4)
 
-        self.opposite = ()
+        self.opposite = (at(y, far(z), x), at(y, z, far(x)))
         self.bits = split_axis(z) + split_axis(x)
         self.partners = (at(y, 3 - z, x), at(y, low(z), x), at(y, z, 3 - x), at(y, z, low(x)))
         if with_dp:
             self.bits = split_axis(y) + self.bits
             self.partners = (at(3 - y, z, x), at(low(y), z, x)) + self.partners
-            self.opposite = tuple(
-                at(*t) for t in ((far(y), z, x), (y, far(z), x), (y, z, far(x))))
+            self.opposite = (at(far(y), z, x),) + self.opposite
         self.dims = len(self.bits)
 
-    def greet(self):
+    def greet(self, others=()):
         barrier = pltpu.get_barrier_semaphore()
-        everyone = (self.sibling,) + self.partners + self.opposite
+        everyone = (self.sibling,) + self.partners + others
         for other in everyone:
             pl.semaphore_signal(barrier, inc=1, device_id=other, device_id_type=MESH)
         pl.semaphore_wait(barrier, len(everyone))
@@ -289,52 +288,71 @@
     return [(start + s) % dims for s in range(dims)]
 
 
+GATHER_PARTS = 8
+
+
 def gather_kernel(k_ref, v_ref, q_ref, do_ref, o_ref, x_ref,
                   k_out, v_out, q_two, do_two, delta_two, xt_two,
-                  k_all, v_all, q_buf, x_buf, do_buf, o_buf, xt_buf, delta_buf,
+                  kv_all, q_buf, x_buf, do_buf, o_buf, xt_buf, delta_buf,
                   hop_send, hop_recv, pass_send, pass_recv, side_send, side_recv, local_sem):
     tok, dim = k_ref.shape
     half = q_two.shape[2]
     here = Place(False)
     c = here.core
     dims = here.dims
-    quarter = tok // dims
-    sources, targets = (k_ref, v_ref), (k_all, v_all)
-
-    own_k, own_v = k_all.at[here.bits + (c,)], v_all.at[here.bits + (c,)]
+    quarter = tok // GATHER_PARTS
+    own = kv_all.at[here.bits + (c,)]
     loads = [
         pltpu.make_async_copy(src, dst, local_sem.at[n])
         for n, (src, dst) in enumerate((
-            (k_ref, own_k), (v_ref, own_v), (q_ref, q_buf), (do_ref, do_buf), (o_ref, o_buf), (x_ref, x_buf)))
+            (k_ref, own.at[0]), (v_ref, own.at[1]), (q_ref, q_buf), (do_ref, do_buf), (o_ref, o_buf), (x_ref, x_buf)))
     ]
     for copy in loads:
         copy.start()
     here.greet()
+    loads[0].wait()
+    loads[1].wait()
 
     def rows(p):
-        return (pl.ds(p * quarter, quarter), slice(None))
-
-    hops = {}
-    for p in range(dims):
-        for kind in range(2):
-            n = (p * dims) * 2 + kind
-            hops[p, 0, kind] = remote(
-                sources[kind].at[rows(p)],
-                targets[kind].at[here.bits + (c,) + rows(p)],
-                hop_send.at[n], hop_recv.at[n], here.partners[turns(dims, p)[0]],
-            )
-            hops[p, 0, kind].start()
+        return (slice(None), pl.ds(p * quarter, quarter), slice(None))
+
+    hops, passes = {}, []
+
+    def hop(p, s):
+        order = turns(dims, p % dims)
+        n = p * dims + s
+        part = kv_all.at[here.spot(order[:s]) + (c,) + rows(p)]
+        hops[p, s] = remote(part, part, hop_send.at[n], hop_recv.at[n], here.partners[order[s]])
+        hops[p, s].start()
+
+    def hand_on(p, s):
+        order = turns(dims, p % dims)
+        n = p * dims + s
+        hops[p, s].wait_recv()
+        part = kv_all.at[here.spot(order[:s], (order[s],)) + (c,) + rows(p)]
+        copy = remote(part, part, pass_send.at[n], pass_recv.at[n], here.sibling)
+        passes.append(copy)
+        return copy
+
+    def next_hop(s):
+        for p in range(GATHER_PARTS):
+            copy = hand_on(p, s)
+            if s < dims - 1:
+                hop(p, s + 1)
+            copy.start()
+
+    for p in range(GATHER_PARTS):
+        hop(p, 0)
     sides = []
     def aside(src, dst):
         n = len(sides)
         sides.append(remote(src, dst, side_send.at[n], side_recv.at[n], here.sibling))
         sides[-1].start()
 
-    for copy in loads[:5]:
+    for copy in loads[2:5]:
         copy.wait()
     theirs, mine = pl.ds((1 - c) * half, half), pl.ds(c * half, half)
-    aside(own_k, own_k)
-    aside(own_v, own_v)
+    aside(own, own)
     aside(q_buf.at[:, theirs], q_two.at[c])
     aside(do_buf.at[:, theirs], do_two.at[c])
     keeps = []
@@ -346,31 +364,7 @@
     keep(q_buf.at[:, mine], q_two.at[c])
     keep(do_buf.at[:, mine], do_two.at[c])
 
-    passes = []
-
-    def hand_on(p, s):
-        order = turns(dims, p)
-        for kind in range(2):
-            n = (p * dims + s) * 2 + kind
-            hops[p, s, kind].wait_recv()
-            part = targets[kind].at[here.spot(order[:s], (order[s],)) + (c,) + rows(p)]
-            copy = remote(part, part, pass_send.at[n], pass_recv.at[n], here.sibling)
-            copy.start()
-            passes.append(copy)
-
-    def hop(p, s):
-        order = turns(dims, p)
-        for kind in range(2):
-            n = (p * dims + s) * 2 + kind
-            part = targets[kind].at[here.spot(order[:s]) + (c,) + rows(p)]
-            hops[p, s, kind] = remote(
-                part, part, hop_send.at[n], hop_recv.at[n], here.partners[order[s]]
-            )
-            hops[p, s, kind].start()
-
-    for p in range(dims):
-        hand_on(p, 0)
-        hop(p, 1)
+    next_hop(0)
     heads = half // dim
     for h in range(2 * heads):
         cols = pl.ds(h * dim, dim)
@@ -387,28 +381,23 @@
         return carry
 
     steps = x_ref.shape[1] // 128
-    for p in range(dims):
-        hand_on(p, 1)
-        hop(p, 2)
+    next_hop(1)
     lax.fori_loop(0, steps // 2, turn, 0)
     mine = xt_two.at[:, pl.ds(c * tok, tok)]
-    for p in range(dims):
-        hand_on(p, 2)
-        hop(p, 3)
+    next_hop(2)
     lax.fori_loop(steps // 2, steps, turn, 0)
     keep(xt_buf, mine)
     aside(xt_buf, mine)
-    for p in range(dims):
-        hand_on(p, 3)
+    next_hop(3)
     everywhere = (slice(None),) * dims
-    keep(k_all.at[everywhere + (c,)], k_out.at[everywhere + (c,)])
-    keep(v_all.at[everywhere + (c,)], v_out.at[everywhere + (c,)])
+    keep(kv_all.at[everywhere + (c, 0)], k_out.at[everywhere + (c,)])
+    keep(kv_all.at[everywhere + (c, 1)], v_out.at[everywhere + (c,)])
     for copy in passes:
         copy.wait()
     for copy in sides:
         copy.wait()
-    keep(k_all.at[everywhere + (1 - c,)], k_out.at[everywhere + (1 - c,)])
-    keep(v_all.at[everywhere + (1 - c,)], v_out.at[everywhere + (1 - c,)])
+    keep(kv_all.at[everywhere + (1 - c, 0)], k_out.at[everywhere + (1 - c,)])
+    keep(kv_all.at[everywhere + (1 - c, 1)], v_out.at[everywhere + (1 - c,)])
     for copy in hops.values():
         copy.wait_send()
     for copy in keeps:
@@ -433,15 +422,14 @@
         in_specs=[anywhere] * 6,
         out_specs=(anywhere,) * 6,
         scratch_shapes=[
-            pltpu.VMEM(full.shape, BF16),
-            pltpu.VMEM(full.shape, BF16),
+            pltpu.VMEM((2, 2, 2, 2, 2, 2, tok, dim), BF16),
             pltpu.VMEM(q.shape, BF16),
             pltpu.VMEM(x.shape, BF16),
             pltpu.VMEM(q.shape, BF16),
             pltpu.VMEM(q.shape, BF16),
             pltpu.VMEM((x.shape[1], tok), BF16),
             pltpu.VMEM((2, 8, tok), F32),
-            dma((32,)), dma((32,)), dma((32,)), dma((32,)), dma((6,)), dma((6,)), dma((14,)),
+            *[dma((4 * GATHER_PARTS,))] * 4, dma((6,)), dma((6,)), dma((14,)),
         ],
         compiler_params=pltpu.CompilerParams(
             collective_id=1, has_side_effects=True, vmem_limit_bytes=59 * 2**20
@@ -458,133 +446,103 @@
     ]
 
 
-def thin_parts(rows, cols):
-    return [(i * (rows // 4), rows // 4, 0, cols) for i in range(4)]
-
-
 def ring_parts(rows, cols):
     half, quarter = rows // 2, rows // 4
     return [(0, half, 0, cols), (half, quarter, 0, cols), (half + quarter, quarter, 0, cols)]
 
 
-class Halving:
-    def __init__(self, here, acc, parts, orders, landing, send, recv):
+def flips(stage):
+    return (stage,) if len(stage) == 1 else (stage, stage[:1], stage[1:])
+
+
+class Sums:
+    def __init__(self, here, acc, parts, orders, landing, sems):
         self.here, self.acc, self.parts, self.orders = here, acc, parts, orders
-        self.landing, self.send_sem, self.recv_sem = landing, send, recv
-        self.copies = {}
-
-    def index(self, p, s, flip):
+        self.send_sem, self.recv_sem = sems
+        self.copies, self.landing = {}, {}
+        for n, key in enumerate(keys(orders)):
+            self.landing[key] = (n, landing[n])
+
+    def index(self, p, s, flipped):
         r0, nr, c0, nc = self.parts[p]
-        order = self.orders[p]
-        free = order[s + 1:]
-        d = order[s]
-        return self.here.spot(free, (d,) if flip else ()) + self.cut(r0, nr, c0, nc)
-
-    def cut(self, r0, nr, c0, nc):
-        return (slice(None),) * (len(self.acc.shape) - self.here.dims - 2) + (
-            pl.ds(r0, nr), pl.ds(c0, nc))
+        free = [d for stage in self.orders[p][s + 1:] for d in stage]
+        if isinstance(self.acc, list):
+            return self.here.spot(free, flipped)
+        middle = (slice(None),) * (len(self.acc.shape) - self.here.dims - 2)
+        return self.here.spot(free, flipped) + middle + (pl.ds(r0, nr), pl.ds(c0, nc))
+
+    def buffer(self, p):
+        return self.acc[p] if isinstance(self.acc, list) else self.acc
 
     def send(self, p, s):
-        dims = self.here.dims
-        n = p * dims + s
-        copy = remote(
-            self.acc.at[self.index(p, s, True)], self.landing[n],
-            self.send_sem.at[n], self.recv_sem.at[n], self.here.partners[self.orders[p][s]],
-        )
-        copy.start()
-        self.copies[p, s] = copy
+        for m, flipped in enumerate(flips(self.orders[p][s])):
+            n, landing = self.landing[p, s, m]
+            partner = self.here.partners[flipped[0]] if len(flipped) == 1 else self.here.opposite[flipped[0] // 2]
+            copy = remote(
+                self.buffer(p).at[self.index(p, s, flipped)], landing, self.send_sem.at[n], self.recv_sem.at[n], partner)
+            copy.start()
+            self.copies[p, s, m] = copy
 
     def total(self, p, s):
-        self.copies[p, s].wait_recv()
-        n = p * self.here.dims + s
-        return self.acc[self.index(p, s, False)].astype(F32) + self.landing[n][...].astype(F32)
-
-    def add(self, p, s):
-        self.acc[self.index(p, s, False)] = self.total(p, s).astype(self.acc.dtype)
+        found = self.buffer(p)[self.index(p, s, ())].astype(F32)
+        for m in range(len(flips(self.orders[p][s]))):
+            self.copies[p, s, m].wait_recv()
+            found = found + self.landing[p, s, m][1][...].astype(F32)
+        return found
+
+    def step(self, s):
+        for p in range(len(self.parts)):
+            self.buffer(p)[self.index(p, s - 1, ())] = self.total(p, s - 1).astype(BF16)
+            self.send(p, s)
 
     def finish(self):
         for copy in self.copies.values():
             copy.wait_send()
 
 
-class Rings:
-    def __init__(self, here, acc, parts, orders, landing, send, recv):
-        self.here, self.acc, self.parts, self.orders = here, acc, parts, orders
-        self.landing, self.send_sem, self.recv_sem = landing, send, recv
-        self.copies = {}
-
-    def index(self, p, s, flipped):
-        r0, nr, c0, nc = self.parts[p]
-        free = [d for a in self.orders[p][s + 1:] for d in (2 * a, 2 * a + 1)]
-        return self.here.spot(free, flipped) + (pl.ds(r0, nr), pl.ds(c0, nc))
-
-    def send(self, p, s):
-        a = self.orders[p][s]
-        high, low = 2 * a, 2 * a + 1
-        ways = (((low,), self.here.partners[low]), ((high,), self.here.partners[high]),
-                ((high, low), self.here.opposite[a]))
-        for m in (2, 0, 1):
-            flipped, partner = ways[m]
-            n = (p * 3 + s) * 3 + m
-            copy = remote(
-                self.acc.at[self.index(p, s, flipped)], self.landing[n],
-                self.send_sem.at[n], self.recv_sem.at[n], partner,
-            )
-            copy.start()
-            self.copies[p, s, m] = copy
-
-    def total(self, p, s):
-        found = self.acc[self.index(p, s, ())].astype(F32)
-        for m in range(3):
-            self.copies[p, s, m].wait_recv()
-            found = found + self.landing[(p * 3 + s) * 3 + m][...].astype(F32)
-        return found
-
-    def add(self, p, s):
-        self.acc[self.index(p, s, ())] = self.total(p, s).astype(self.acc.dtype)
-
-    def finish(self):
-        for copy in self.copies.values():
-            copy.wait_send()
-
-
-def ring_shapes(parts):
-    return [(2,) * (2 * (2 - s)) + (nr, nc) for (_, nr, _, nc) in parts for s in range(3) for _ in range(3)]
+def keys(orders):
+    return [(p, s, m) for p, order in enumerate(orders) for s, stage in enumerate(order)
+            for m in range(len(flips(stage)))]
 
 
 def landing_shapes(parts, orders, extra):
     shapes = []
-    for (_, nr, _, nc), order in zip(parts, orders):
-        for s in range(len(order)):
-            shapes.append((2,) * (len(order) - 1 - s) + extra + (nr, nc))
+    for p, s, _ in keys(orders):
+        left = sum(len(stage) for stage in orders[p][s + 1:])
+        shapes.append((2,) * left + extra + (parts[p][1], parts[p][3]))
     return shapes
 
 
 def layout(tok, dim, half, features):
     row_chunk = features // 64
-    kv_parts = thin_parts(tok, dim)
-    kv_orders = [turns(4, p) for p in range(4)]
+    kv_parts = [(i * (tok // 8), tok // 8, 0, dim) for i in range(8)]
+    kv_orders = [
+        ((0,), (1,), (2, 3)), ((1,), (0,), (2, 3)), ((2,), (3,), (0, 1)), ((3,), (2,), (0, 1))] * 2
     wide = wide_parts(row_chunk, half)
-    wide_orders = [turns(6, p) for p in range(6)]
+    wide_orders = [
+        ((0,), (1,), (2, 3), (4, 5)), ((1,), (0,), (4, 5), (2, 3)), ((2,), (3,), (4, 5), (0, 1)),
+        ((3,), (2,), (0, 1), (4, 5)), ((4,), (5,), (0, 1), (2, 3)), ((5,), (4,), (2, 3), (0, 1))]
     thin = ring_parts(row_chunk, dim)
-    thin_orders = [turns(3, p) for p in range(3)]
+    thin_orders = [
+        ((0, 1), (2, 3), (4, 5)), ((2, 3), (4, 5), (0, 1)), ((4, 5), (0, 1), (2, 3))]
     return row_chunk, kv_parts, kv_orders, wide, wide_orders, thin, thin_orders
 
 
 def reduce_kernel(plan, scale, dkv_ref, dq_ref, xt_ref, qg_ref, kvg_ref, wg_ref, *scratch):
     row_chunk, kv_parts, kv_orders, wide, wide_orders, thin, thin_orders = plan
-    (kv_acc, kv_in, kv_mine, w_acc, t_acc, xt, dq, fin, kv_send, kv_recv, w_send, w_recv, t_send, t_recv,
-     side_send, side_recv, local_sem) = scratch[:17]
-    landing = scratch[17:]
+    (kv_acc, kv_in, kv_mine, t_acc, xt, dq, fin, kv_send, kv_recv, w_send, w_recv, t_send, t_recv,
+     side_send, side_recv, local_sem) = scratch[:16]
+    w_acc = list(scratch[16:16 + len(wide)])
+    landing = scratch[16 + len(wide):]
     tok, dim = dkv_ref.shape[-2:]
     half = dq_ref.shape[2]
     here_w = Place(True)
     here = Place(False)
     c = here.core
-    n_kv, n_w = 16, 36
-    kv = Halving(here, kv_acc, kv_parts, kv_orders, landing[:n_kv], kv_send, kv_recv)
-    w = Halving(here_w, w_acc, wide, wide_orders, landing[n_kv:n_kv + n_w], w_send, w_recv)
-    t = Rings(here_w, t_acc, thin, thin_orders, landing[n_kv + n_w:], t_send, t_recv)
+    n_kv, n_w = len(keys(kv_orders)), len(keys(wide_orders))
+    kv = Sums(here, kv_acc, kv_parts, kv_orders, landing[:n_kv], (kv_send, kv_recv))
+    w = Sums(here_w, w_acc, wide, wide_orders, landing[n_kv:n_kv + n_w], (w_send, w_recv))
+    t = Sums(here_w, t_acc, thin, thin_orders, landing[n_kv + n_w:], (t_send, t_recv))
 
     load_x = pltpu.make_async_copy(xt_ref, xt, local_sem.at[1])
     load_x.start()
@@ -592,7 +550,7 @@
     load_q.start()
     load_kv = pltpu.make_async_copy(dkv_ref.at[c], kv_acc, local_sem.at[2])
     load_kv.start()
-    here_w.greet()
+    here_w.greet(here_w.opposite)
     sides = []
 
     def aside(src, dst):
@@ -601,32 +559,20 @@
         sides[-1].start()
 
     rest = (slice(None),) * 5
-    for p in range(4):
+    for p in range(len(kv_parts)):
         r0, nr, _, _ = kv_parts[p]
         aside(dkv_ref.at[(1 - c,) + rest + (pl.ds(r0, nr),)], kv_in.at[rest + (pl.ds(r0, nr),)])
     aside(dq_ref.at[1 - c], qg_ref.at[:, pl.ds(c * half, half)])
 
-    load_kv.wait()
-    for p in range(4):
-        r0, nr, _, _ = kv_parts[p]
-        sides[p].wait_recv()
-
-        def join(i, carry, r0=r0, nr=nr):
-            at = (i // 8, lax.rem(i // 4, 2), lax.rem(i // 2, 2), lax.rem(i, 2), slice(None), pl.ds(r0, nr))
-            kv_acc[at] = (kv_acc[at].astype(F32) + kv_in[at].astype(F32)).astype(BF16)
-            return carry
-
-        lax.fori_loop(0, 16, join, 0)
-        kv.send(p, 0)
-
-    def products(i, right, acc):
+    def products(i, right, accs, parts):
         block = dot(xt[pl.ds(i * 8 * row_chunk, 8 * row_chunk), :], right).astype(BF16)
         y = i // 2
         for j in range(8):
             z = 2 * lax.rem(i, 2) + j // 4
             x = j % 4
             at = split_axis(y) + split_axis(z) + (x // 2, (x + x // 2) % 2)
-            acc[at] = block[j * row_chunk:(j + 1) * row_chunk]
+            for acc, (r0, nr, c0, nc) in zip(accs, parts):
+                acc[at] = block[j * row_chunk + r0:j * row_chunk + r0 + nr, c0:c0 + nc]
 
     load_x.wait()
     load_q.wait()
@@ -635,66 +581,72 @@
     both = dq[...].reshape(2 * tok, half)
 
     def wide_products(i, carry):
-        products(i, both, w_acc)
+        products(i, both, w_acc, wide)
         return carry
 
     lax.fori_loop(0, 8, wide_products, 0)
-    for p in range(6):
+    load_kv.wait()
+    for p in range(len(kv_parts)):
+        r0, nr, _, _ = kv_parts[p]
+        sides[p].wait_recv()
+
+        def join(i, carry, r0=r0, nr=nr):
+            at = (i // 8, lax.rem(i // 4, 2), lax.rem(i // 2, 2), lax.rem(i, 2), slice(None), pl.ds(r0, nr))
+            kv_acc[at] = (kv_acc[at].astype(F32) + kv_in[at].astype(F32)).astype(BF16)
+            return carry
+
+        lax.fori_loop(0, 16, join, 0)
+        kv.send(p, 0)
+
+    for p in range(len(wide)):
         w.send(p, 0)
-    def wide_step(s):
-        for p in range(6):
-            w.add(p, s - 1)
-            w.send(p, s)
-
-    for s in range(1, 4):
-        for p in range(4):
-            kv.add(p, s - 1)
-            kv.send(p, s)
-        if s > 1:
-            wide_step(s - 1)
+    kv.step(1)
+    kv.step(2)
+    w.step(1)
     kv_scale = jnp.where(c == 0, scale, 1.0).astype(F32)
-    for p in range(4):
+    for p in range(len(kv_parts)):
         r0, nr, _, _ = kv_parts[p]
-        kv_mine[:, pl.ds(r0, nr), :] = (kv.total(p, 3) * kv_scale).astype(BF16)
+        kv_mine[:, pl.ds(r0, nr), :] = (kv.total(p, 2) * kv_scale).astype(BF16)
     own_kv = pltpu.make_async_copy(kv_mine.at[c], kvg_ref.at[c], local_sem.at[4])
     own_kv.start()
     aside(kv_mine.at[1 - c], kvg_ref.at[c])
     mine = kv_mine[...].reshape(2 * tok, dim)
 
     def thin_products(i, carry):
-        products(i, mine, t_acc)
+        products(i, mine, [t_acc], [(0, row_chunk, 0, dim)])
         return carry
 
     lax.fori_loop(0, 8, thin_products, 0)
-    for p in range(3):
+    for p in range(len(thin)):
         t.send(p, 0)
-    wide_step(3)
-    for s in range(1, 3):
-        for p in range(3):
-            t.add(p, s - 1)
-            t.send(p, s)
-        wide_step(s + 3)
-    for p, (r0, nr, c0, nc) in enumerate(wide):
-        fin[pl.ds(r0, nr), pl.ds(c0, nc)] = w.total(p, 5)
-    for p, (r0, nr, c0, nc) in enumerate(thin):
-        fin[pl.ds(r0, nr), pl.ds(half, nc)] = t.total(p, 2)
+    w.step(2)
+    t.step(1)
+    w.step(3)
+    t.step(2)
     rows_out = row_chunk // 2
-    pieces = [(0, c * half, half), (half, 2 * half + c * dim, dim)]
     own_w = []
-    for n, (src, dst, width) in enumerate(pieces):
+
+    def hand_out(src, dst, width):
         own_w.append(pltpu.make_async_copy(
             fin.at[pl.ds(c * rows_out, rows_out), pl.ds(src, width)],
-            wg_ref.at[:, pl.ds(dst, width)], local_sem.at[5 + n]))
+            wg_ref.at[:, pl.ds(dst, width)], local_sem.at[5 + len(own_w)]))
         own_w[-1].start()
         aside(fin.at[pl.ds((1 - c) * rows_out, rows_out), pl.ds(src, width)],
               wg_ref.at[:, pl.ds(dst, width)])
+
+    for p, (r0, nr, c0, nc) in enumerate(wide):
+        fin[pl.ds(r0, nr), pl.ds(c0, nc)] = w.total(p, 3)
+    hand_out(0, c * half, half)
+    for p, (r0, nr, c0, nc) in enumerate(thin):
+        fin[pl.ds(r0, nr), pl.ds(half, nc)] = t.total(p, 2)
+    hand_out(half, 2 * half + c * dim, dim)
     own_q.wait()
     own_kv.wait()
     for copy in own_w:
         copy.wait()
     for n, copy in enumerate(sides):
         copy.wait_send()
-        if n >= 4:
+        if n >= len(kv_parts):
             copy.wait_recv()
     kv.finish()
     w.finish()
@@ -709,7 +661,7 @@
     row_chunk, kv_parts, kv_orders, wide, wide_orders, thin, thin_orders = plan
     dma = pltpu.SemaphoreType.DMA
     shapes = (landing_shapes(kv_parts, kv_orders, (2,)) + landing_shapes(wide, wide_orders, ())
-              + ring_shapes(thin))
+              + landing_shapes(thin, thin_orders, ()))
     return pl.pallas_call(
         functools.partial(reduce_kernel, plan, scale),
         out_shape=(
@@ -723,14 +675,14 @@
             pltpu.VMEM(dkv.shape[1:], BF16),
             pltpu.VMEM(dkv.shape[1:], BF16),
             pltpu.VMEM((2, tok, dim), BF16),
-            pltpu.VMEM((2,) * 6 + (row_chunk, half), BF16),
             pltpu.VMEM((2,) * 6 + (row_chunk, dim), BF16),
             pltpu.VMEM(xt.shape, BF16),
             pltpu.VMEM(dq.shape, BF16),
             pltpu.VMEM((row_chunk, half + dim), F32),
-            dma((16,)), dma((16,)), dma((36,)), dma((36,)), dma((27,)), dma((27,)),
-            dma((8,)), dma((8,)), dma((8,)),
-        ] + [pltpu.VMEM(shape, BF16) for shape in shapes],
+            *[dma((len(keys(orders)),)) for orders in (kv_orders, wide_orders, thin_orders) for _ in range(2)],
+            dma((12,)), dma((12,)), dma((8,)),
+        ] + [pltpu.VMEM((2,) * 6 + (nr, nc), BF16) for _, nr, _, nc in wide]
+        + [pltpu.VMEM(shape, BF16) for shape in shapes],
         compiler_params=pltpu.CompilerParams(
             collective_id=2, has_side_effects=True, vmem_limit_bytes=58 * 2**20
         ),

time: 126 us -> 119 us (0.944)
  Pallas kernels: 125 us -> 118 us
    pallas_call x1, Pallas kernels: 68.4 us -> 64.5 us  [reduce(): pl.pallas_call(functools.partial(reduce_kernel, plan, scale), out_shape=(...]
    pallas_call x1, Pallas kernels: 25 us -> 22.8 us  [attention(): pl.pallas_call(functools.partial(attention_kernel, sets, heads, tok, dim,...]
where the time goes in v6:
time: 119 us
  Pallas kernels  118 us (99%)
    pallas_call x1, Pallas kernels, reduce(): pl.pallas_call(functools.partial(reduce_kernel, plan, scale), out_shape=(...  64.5 us
    pallas_call x1, Pallas kernels, gather(): pl.pallas_call(gather_kernel, out_shape=(full, full, jax.ShapeDtypeStruct...  28.9 us
    pallas_call x1, Pallas kernels, attention(): pl.pallas_call(functools.partial(attention_kernel, sets, heads, tok, dim,...  22.8 us

profile of v6, /device:TPU:1, one launch (start us, length us, event | category | flops | bytes accessed | tf_op | source)
XLA Modules:
  0.0 118.9 jit_solution(8206628762515460457)
XLA Ops:
  0.6 28.9 %gather.1 = (bf16[2,2,2,2,2,256,128]{6,5,4,3,2,1,0:T(8,128)(2,1)}, bf16[2,2,2,2,2,256,128]{6,5,4,3,2,1,0:T(8,128)(2,1)}, bf16[2,256,512]{2,1,0:T(8,128)(2,1)}, b...) custom-call(bf16[256,128]{1,0:T(8,128)(2,1)} %bitcast.16, bf16[256,128]{1,0:T(8,128)(2,1)} %bitcast.17, ...), custom_call_target="tpu_custom_call" | custom-call | tf_op jit(solution)/shard_map/gather/pallas_call | solution.py:413
  29.5 22.8 %attention.1 = (bf16[2,256,512]{2,1,0:T(8,128)(2,1)}, bf16[2,32,256,128]{3,2,1,0:T(8,128)(2,1)}) custom-call(s32[1,4]{1,0:T(1,128)} %lengths_ref.1, s32[1,32]{1,0:T(1,128)} %span_ref.1, bf16[2,256,512]{2,1,0:T(8,128)(2,1)} %get-tuple-element.15.q_in, bf16[2,256,512]{2,1,0:T(8,128)(2,1)} %get-tuple-element.16.do_in, f32[2,8,256]{2,1,0:T(8,128)} %get-tuple-element.17.delta_in, ...), custom_call_target="tpu_custom_call" | custom-call | tf_op jit(solution)/shard_map/attention/pallas_call | solution.py:192
  52.3 64.5 %reduce.1 = (bf16[256,1024]{1,0:T(8,128)(2,1)}, bf16[2,256,128]{2,1,0:T(8,128)(2,1)}, f32[32,1280]{1,0:T(8,128)}) custom-call(bf16[2,2,2,2,2,2,256,128]{7,6,5,4,3,2,1,0:T(8,128)(2,1)} %bitcast.9, bf16[2,256,512]{2,1,0:T(8,128)(2,1)} %get-tuple-element.21.dq_ref, bf16[4096,512]{1,0:T(8,128)(2,1)} %get-tuple-element.22.xt_ref), custom_call_target="tpu_custom_call" | custom-call | tf_op jit(solution)/shard_map/reduce/pallas_call | solution.py:665
  116.9 2.1 %finish.1 = (bf16[1,256,1024]{2,1,0:T(8,128)(2,1)}, bf16[1,256,128]{2,1,0:T(8,128)(2,1)}, bf16[1,256,128]{2,1,0:T(8,128)(2,1)}, f32[32,1280]{1,0:T(8,128)}) custom-call(bf16[256,1024]{1,0:T(8,128)(2,1)} %get-tuple-element.23.qg_ref, bf16[2,256,128]{2,1,0:T(8,128)(2,1)} %get-tuple-element.24.kvg_ref, f32[32,1280]{1,0:T(8,128)} %get-tuple-element.25.wg_ref), custom_call_target="tpu_custom_call" | custom-call | tf_op jit(solution)/shard_map/finish/pallas_call | solution.py:705

commit v7 on v6

--- a/solution.py
+++ b/solution.py
@@ -439,10 +439,10 @@
 
 
 def wide_parts(rows, cols):
-    cut = cols // 4 * 3
+    cut = cols // 2
     quarter, half = rows // 4, rows // 2
-    return [(i * quarter, quarter, 0, cut) for i in range(4)] + [
-        (i * half, half, cut, cols - cut) for i in range(2)
+    return [(i * half, half, 0, cut) for i in range(2)] + [
+        (i * quarter, quarter, cut, cols - cut) for i in range(4)
     ]
 
 
@@ -585,6 +585,8 @@
         return carry
 
     lax.fori_loop(0, 8, wide_products, 0)
+    for p in range(2):
+        w.send(p, 0)
     load_kv.wait()
     for p in range(len(kv_parts)):
         r0, nr, _, _ = kv_parts[p]
@@ -598,9 +600,9 @@
         lax.fori_loop(0, 16, join, 0)
         kv.send(p, 0)
 
-    for p in range(len(wide)):
+    kv.step(1)
+    for p in range(2, len(wide)):
         w.send(p, 0)
-    kv.step(1)
     kv.step(2)
     w.step(1)
     kv_scale = jnp.where(c == 0, scale, 1.0).astype(F32)

time: 119 us -> 120 us (level)
    pallas_call x1, Pallas kernels: 64.5 us -> 67.1 us  [reduce(): pl.pallas_call(functools.partial(reduce_kernel, plan, scale), out_shape=(...]
    pallas_call x1, Pallas kernels: 22.8 us -> 20.5 us  [attention(): pl.pallas_call(functools.partial(attention_kernel, sets, heads, tok, dim,...]
where the time goes in v7:
time: 120 us; the launch traced here: 119 us
  Pallas kernels  119 us (99%)
    pallas_call x1, Pallas kernels, reduce(): pl.pallas_call(functools.partial(reduce_kernel, plan, scale), out_shape=(...  67.1 us
    pallas_call x1, Pallas kernels, gather(): pl.pallas_call(gather_kernel, out_shape=(full, full, jax.ShapeDtypeStruct...  28.9 us
    pallas_call x1, Pallas kernels, attention(): pl.pallas_call(functools.partial(attention_kernel, sets, heads, tok, dim,...  20.5 us

profile of v7, /device:TPU:1, one launch (start us, length us, event | category | flops | bytes accessed | tf_op | source)
XLA Modules:
  0.0 119.2 jit_solution(6200050582657877537)
XLA Ops:
  0.6 28.9 %gather.1 = (bf16[2,2,2,2,2,256,128]{6,5,4,3,2,1,0:T(8,128)(2,1)}, bf16[2,2,2,2,2,256,128]{6,5,4,3,2,1,0:T(8,128)(2,1)}, bf16[2,256,512]{2,1,0:T(8,128)(2,1)}, b...) custom-call(bf16[256,128]{1,0:T(8,128)(2,1)} %bitcast.16, bf16[256,128]{1,0:T(8,128)(2,1)} %bitcast.17, ...), custom_call_target="tpu_custom_call" | custom-call | tf_op jit(solution)/shard_map/gather/pallas_call | solution.py:413
  29.5 20.5 %attention.1 = (bf16[2,256,512]{2,1,0:T(8,128)(2,1)}, bf16[2,32,256,128]{3,2,1,0:T(8,128)(2,1)}) custom-call(s32[1,4]{1,0:T(1,128)} %lengths_ref.1, s32[1,32]{1,0:T(1,128)} %span_ref.1, bf16[2,256,512]{2,1,0:T(8,128)(2,1)} %get-tuple-element.15.q_in, bf16[2,256,512]{2,1,0:T(8,128)(2,1)} %get-tuple-element.16.do_in, f32[2,8,256]{2,1,0:T(8,128)} %get-tuple-element.17.delta_in, ...), custom_call_target="tpu_custom_call" | custom-call | tf_op jit(solution)/shard_map/attention/pallas_call | solution.py:192
  50.0 67.1 %reduce.1 = (bf16[256,1024]{1,0:T(8,128)(2,1)}, bf16[2,256,128]{2,1,0:T(8,128)(2,1)}, f32[32,1280]{1,0:T(8,128)}) custom-call(bf16[2,2,2,2,2,2,256,128]{7,6,5,4,3,2,1,0:T(8,128)(2,1)} %bitcast.9, bf16[2,256,512]{2,1,0:T(8,128)(2,1)} %get-tuple-element.21.dq_ref, bf16[4096,512]{1,0:T(8,128)(2,1)} %get-tuple-element.22.xt_ref), custom_call_target="tpu_custom_call" | custom-call | tf_op jit(solution)/shard_map/reduce/pallas_call | solution.py:667
  117.1 2.1 %finish.1 = (bf16[1,256,1024]{2,1,0:T(8,128)(2,1)}, bf16[1,256,128]{2,1,0:T(8,128)(2,1)}, bf16[1,256,128]{2,1,0:T(8,128)(2,1)}, f32[32,1280]{1,0:T(8,128)}) custom-call(bf16[256,1024]{1,0:T(8,128)(2,1)} %get-tuple-element.23.qg_ref, bf16[2,256,128]{2,1,0:T(8,128)(2,1)} %get-tuple-element.24.kvg_ref, f32[32,1280]{1,0:T(8,128)} %get-tuple-element.25.wg_ref), custom_call_target="tpu_custom_call" | custom-call | tf_op jit(solution)/shard_map/finish/pallas_call | solution.py:707

commit v8 on v7

--- a/solution.py
+++ b/solution.py
@@ -266,6 +266,9 @@
             pl.semaphore_signal(barrier, inc=1, device_id=other, device_id_type=MESH)
         pl.semaphore_wait(barrier, len(everyone))
 
+    def partner(self, flipped):
+        return self.partners[flipped[0]] if len(flipped) == 1 else self.opposite[flipped[0] // 2]
+
     def spot(self, free, flipped=()):
         found = []
         for d in range(self.dims):
@@ -289,6 +292,8 @@
 
 
 GATHER_PARTS = 8
+GATHER_ORDERS = (
+    ((2, 3), (0,), (1,)), ((2, 3), (1,), (0,)), ((0, 1), (2,), (3,)), ((0, 1), (3,), (2,)))
 
 
 def gather_kernel(k_ref, v_ref, q_ref, do_ref, o_ref, x_ref,
@@ -309,7 +314,7 @@
     ]
     for copy in loads:
         copy.start()
-    here.greet()
+    here.greet(here.opposite)
     loads[0].wait()
     loads[1].wait()
 
@@ -318,28 +323,29 @@
 
     hops, passes = {}, []
 
+    def held(p, s, flipped=()):
+        free = [d for stage in GATHER_ORDERS[p % dims][:s] for d in stage]
+        return kv_all.at[here.spot(free, flipped) + (c,) + rows(p)]
+
     def hop(p, s):
-        order = turns(dims, p % dims)
-        n = p * dims + s
-        part = kv_all.at[here.spot(order[:s]) + (c,) + rows(p)]
-        hops[p, s] = remote(part, part, hop_send.at[n], hop_recv.at[n], here.partners[order[s]])
-        hops[p, s].start()
-
-    def hand_on(p, s):
-        order = turns(dims, p % dims)
-        n = p * dims + s
-        hops[p, s].wait_recv()
-        part = kv_all.at[here.spot(order[:s], (order[s],)) + (c,) + rows(p)]
-        copy = remote(part, part, pass_send.at[n], pass_recv.at[n], here.sibling)
-        passes.append(copy)
-        return copy
+        for m, flipped in enumerate(flips(GATHER_ORDERS[p % dims][s])):
+            n = p * 5 + (m if s == 0 else s + 2)
+            part = held(p, s)
+            hops[p, s, m] = remote(part, part, hop_send.at[n], hop_recv.at[n], here.partner(flipped))
+            hops[p, s, m].start()
 
     def next_hop(s):
         for p in range(GATHER_PARTS):
-            copy = hand_on(p, s)
-            if s < dims - 1:
+            ways = flips(GATHER_ORDERS[p % dims][s])
+            for m in range(len(ways)):
+                hops[p, s, m].wait_recv()
+            if s < 2:
                 hop(p, s + 1)
-            copy.start()
+            for m, flipped in enumerate(ways):
+                n = p * 5 + (m if s == 0 else s + 2)
+                part = held(p, s, flipped)
+                passes.append(remote(part, part, pass_send.at[n], pass_recv.at[n], here.sibling))
+                passes[-1].start()
 
     for p in range(GATHER_PARTS):
         hop(p, 0)
@@ -382,13 +388,11 @@
 
     steps = x_ref.shape[1] // 128
     next_hop(1)
-    lax.fori_loop(0, steps // 2, turn, 0)
     mine = xt_two.at[:, pl.ds(c * tok, tok)]
-    next_hop(2)
-    lax.fori_loop(steps // 2, steps, turn, 0)
+    lax.fori_loop(0, steps, turn, 0)
     keep(xt_buf, mine)
     aside(xt_buf, mine)
-    next_hop(3)
+    next_hop(2)
     everywhere = (slice(None),) * dims
     keep(kv_all.at[everywhere + (c, 0)], k_out.at[everywhere + (c,)])
     keep(kv_all.at[everywhere + (c, 1)], v_out.at[everywhere + (c,)])
@@ -429,7 +433,7 @@
             pltpu.VMEM(q.shape, BF16),
             pltpu.VMEM((x.shape[1], tok), BF16),
             pltpu.VMEM((2, 8, tok), F32),
-            *[dma((4 * GATHER_PARTS,))] * 4, dma((6,)), dma((6,)), dma((14,)),
+            *[dma((5 * GATHER_PARTS,))] * 4, dma((6,)), dma((6,)), dma((14,)),
         ],
         compiler_params=pltpu.CompilerParams(
             collective_id=1, has_side_effects=True, vmem_limit_bytes=59 * 2**20
@@ -477,7 +481,7 @@
     def send(self, p, s):
         for m, flipped in enumerate(flips(self.orders[p][s])):
             n, landing = self.landing[p, s, m]
-            partner = self.here.partners[flipped[0]] if len(flipped) == 1 else self.here.opposite[flipped[0] // 2]
+            partner = self.here.partner(flipped)
             copy = remote(
                 self.buffer(p).at[self.index(p, s, flipped)], landing, self.send_sem.at[n], self.recv_sem.at[n], partner)
             copy.start()

time: 120 us -> 120 us (level); the launches traced: 119 us -> 121 us
    pallas_call x1, Pallas kernels: 67.1 us -> 73 us  [reduce(): pl.pallas_call(functools.partial(reduce_kernel, plan, scale), out_shape=(...]
    pallas_call x1, Pallas kernels: 20.5 us -> 18.2 us  [attention(): pl.pallas_call(functools.partial(attention_kernel, sets, heads, tok, dim,...]
    pallas_call x1, Pallas kernels: 28.9 us -> 26.7 us  [gather(): pl.pallas_call(gather_kernel, out_shape=(full, full, jax.ShapeDtypeStruct...]
where the time goes in v8:
time: 120 us; the launch traced here: 121 us
  Pallas kernels  120 us (100%)
    pallas_call x1, Pallas kernels, reduce(): pl.pallas_call(functools.partial(reduce_kernel, plan, scale), out_shape=(...  73 us
    pallas_call x1, Pallas kernels, gather(): pl.pallas_call(gather_kernel, out_shape=(full, full, jax.ShapeDtypeStruct...  26.7 us
    pallas_call x1, Pallas kernels, attention(): pl.pallas_call(functools.partial(attention_kernel, sets, heads, tok, dim,...  18.2 us

profile of v8, /device:TPU:1, one launch (start us, length us, event | category | flops | bytes accessed | tf_op | source)
XLA Modules:
  0.0 120.6 jit_solution(6305148683284466565)
XLA Ops:
  0.6 26.7 %gather.1 = (bf16[2,2,2,2,2,256,128]{6,5,4,3,2,1,0:T(8,128)(2,1)}, bf16[2,2,2,2,2,256,128]{6,5,4,3,2,1,0:T(8,128)(2,1)}, bf16[2,256,512]{2,1,0:T(8,128)(2,1)}, b...) custom-call(bf16[256,128]{1,0:T(8,128)(2,1)} %bitcast.16, bf16[256,128]{1,0:T(8,128)(2,1)} %bitcast.17, ...), custom_call_target="tpu_custom_call" | custom-call | tf_op jit(solution)/shard_map/gather/pallas_call | solution.py:417
  27.4 18.2 %attention.1 = (bf16[2,256,512]{2,1,0:T(8,128)(2,1)}, bf16[2,32,256,128]{3,2,1,0:T(8,128)(2,1)}) custom-call(s32[1,4]{1,0:T(1,128)} %lengths_ref.1, s32[1,32]{1,0:T(1,128)} %span_ref.1, bf16[2,256,512]{2,1,0:T(8,128)(2,1)} %get-tuple-element.15.q_in, bf16[2,256,512]{2,1,0:T(8,128)(2,1)} %get-tuple-element.16.do_in, f32[2,8,256]{2,1,0:T(8,128)} %get-tuple-element.17.delta_in, ...), custom_call_target="tpu_custom_call" | custom-call | tf_op jit(solution)/shard_map/attention/pallas_call | solution.py:192
  45.6 73.0 %reduce.1 = (bf16[256,1024]{1,0:T(8,128)(2,1)}, bf16[2,256,128]{2,1,0:T(8,128)(2,1)}, f32[32,1280]{1,0:T(8,128)}) custom-call(bf16[2,2,2,2,2,2,256,128]{7,6,5,4,3,2,1,0:T(8,128)(2,1)} %bitcast.9, bf16[2,256,512]{2,1,0:T(8,128)(2,1)} %get-tuple-element.21.dq_ref, bf16[4096,512]{1,0:T(8,128)(2,1)} %get-tuple-element.22.xt_ref), custom_call_target="tpu_custom_call" | custom-call | tf_op jit(solution)/shard_map/reduce/pallas_call | solution.py:671
  118.6 2.1 %finish.1 = (bf16[1,256,1024]{2,1,0:T(8,128)(2,1)}, bf16[1,256,128]{2,1,0:T(8,128)(2,1)}, bf16[1,256,128]{2,1,0:T(8,128)(2,1)}, f32[32,1280]{1,0:T(8,128)}) custom-call(bf16[256,1024]{1,0:T(8,128)(2,1)} %get-tuple-element.23.qg_ref, bf16[2,256,128]{2,1,0:T(8,128)(2,1)} %get-tuple-element.24.kvg_ref, f32[32,1280]{1,0:T(8,128)} %get-tuple-element.25.wg_ref), custom_call_target="tpu_custom_call" | custom-call | tf_op jit(solution)/shard_map/finish/pallas_call | solution.py:711
